TPU v7x, 512 devices: a whole 4x4x16 slice. The times are simulated.
512 devices in a mesh: lon: 64 (over x_lo, z, core), lat: 8 (over y, x_hi).
Axes of the slice: x: 4 (x_hi: 2, x_lo: 2; x = x_hi * 2 + x_lo), y: 4, z: 16, core: 2. Of those that a mesh axis runs over, the one named last changes fastest.
Arguments:
- state_in: bfloat16 [8, 48, 147456], P(None, 'lat', 'lon'), may hold values from -60 to 60
- cotangent: bfloat16 [8, 48, 147456], P(None, 'lat', 'lon'), may hold values from -6 to 6
- w_qkv: bfloat16 [192, 576], replicated, may hold values from -0.4375 to 0.4375
- w_proj: bfloat16 [192, 192], replicated, may hold values from -0.4375 to 0.4375
- w_up: bfloat16 [192, 768], replicated, may hold values from -0.4375 to 0.4375
- w_down: bfloat16 [768, 192], replicated, may hold values from -0.21875 to 0.21875
- bias_table: float32 [32, 19872], P('lat'), may hold values from -4 to 300
- pad_valid: int32 [768], P('lon'), may hold values from 0 to 1, as said below
Outputs:
- grad_input: bfloat16 [8, 48, 147456], P(None, 'lat', 'lon')
- grad_qkv: float32 [192, 576], replicated
- grad_proj: float32 [192, 192], replicated
- grad_up: float32 [192, 768], replicated
- grad_down: float32 [768, 192], replicated
- grad_table: float32 [32, 19872], P('lat')
Inputs may be any that keep to these rules, and one draw needn't show every extreme that they name: `pad_valid`: exactly 168 columns are 0, and they form one contiguous run around the longitude loop.
All inputs are finite; a program needn't handle non-finite values.
Results may differ from a plain program's by a relative error of at most 0.017.
Values may be sent and summed in bfloat16 or wider, within the bound.
A program may use at most 64 MiB of HBM per device.

v0:
```python
import jax
import jax.numpy as jnp
from jax import lax
from jax.sharding import PartitionSpec as P

HEADS = 6
WZ = 2
WH = 6
WW = 12


MASKED_SCORE = -1e30
NORM_EPS = 1e-05


def passed_along(value, axis, steps):
    count = lax.axis_size(axis)
    pairs = [(source, (source + steps) % count) for source in range(count)]
    return lax.ppermute(value, axis, pairs)


def shortened(value):
    return jax.tree.map(lambda a: a.astype(jnp.bfloat16) if a.dtype == jnp.float32 else a, value)


def layer_norm(inputs):
    average = jnp.mean(inputs, axis=-1, keepdims=True)
    centred = inputs - average
    inv_std = lax.rsqrt(jnp.mean(centred * centred, axis=-1, keepdims=True) + NORM_EPS)
    return (centred * inv_std, inv_std)


def norm_back(upstream, normed, inv_std):
    return inv_std * (
        upstream
        - jnp.mean(upstream, axis=-1, keepdims=True)
        - normed * jnp.mean(upstream * normed, axis=-1, keepdims=True)
    )


def gelu_exact(inputs):
    return 0.5 * inputs * (1.0 + lax.erf(inputs * 0.7071067811865476))


def gelu_slope(inputs):
    return (
        0.5 * (1.0 + lax.erf(inputs * 0.7071067811865476))
        + inputs * jnp.exp(-0.5 * inputs * inputs) * 0.3989422804014327
    )


def flat_dot(left_op, right_op):
    flat = left_op.reshape(-1, left_op.shape[-1])
    product = jnp.dot(flat, right_op, preferred_element_type=jnp.float32)
    return product.reshape(left_op.shape[:-1] + (right_op.shape[-1],))


def grad_dot(left_op, right_op):
    return jnp.dot(
        left_op.reshape(-1, left_op.shape[-1]).T,
        right_op.reshape(-1, right_op.shape[-1]),
        preferred_element_type=jnp.float32,
    )


def batched(formula, left_op, right_op):
    return jnp.einsum(formula, left_op, right_op, preferred_element_type=jnp.float32)


def spread_table():
    span = 2 * WW - 1
    row_level = jnp.arange(WZ)[:, None, None, None, None, None, None]
    row_lat = jnp.arange(WH)[None, :, None, None, None, None, None]
    row_off = jnp.arange(span)[None, None, :, None, None, None, None]
    col_query = jnp.arange(WW)[None, None, None, :, None, None, None]
    col_level = jnp.arange(WZ)[None, None, None, None, :, None, None]
    col_lat = jnp.arange(WH)[None, None, None, None, None, :, None]
    col_key = jnp.arange(WW)[None, None, None, None, None, None, :]
    hit = (
        (row_level == col_level) & (row_lat == col_lat) & (row_off == col_query - col_key + WW - 1)
    )
    return hit.astype(jnp.float32).reshape(WZ * WH * span, WW * WZ * WH * WW)


def window_bias(bias_rows):
    window_count = bias_rows.shape[0]
    span = 2 * WW - 1
    grid = bias_rows.reshape(window_count, HEADS, WZ, WZ, WH, WH, span).transpose(
        0, 1, 2, 4, 3, 5, 6
    )
    grid = grid.reshape(window_count * HEADS * WZ * WH, WZ * WH * span)
    spread = jnp.dot(grid, spread_table(), precision=lax.Precision.HIGHEST)
    window_cells = WZ * WH * WW
    return spread.reshape(window_count, HEADS, window_cells, window_cells)


def bias_grad(dscore):
    window_count = dscore.shape[0]
    span = 2 * WW - 1
    flat = dscore.reshape(window_count * HEADS * WZ * WH, WW * WZ * WH * WW)
    grid = jnp.dot(flat, spread_table().T, precision=lax.Precision.HIGHEST)
    grid = grid.reshape(window_count, HEADS, WZ, WH, WZ, WH, span).transpose(0, 1, 2, 4, 3, 5, 6)
    return grid.reshape(window_count, HEADS * WZ * WZ * WH * WH * span)


def to_windows(field_in):
    z_windows = field_in.shape[0] // WZ
    h_windows = field_in.shape[1] // WH
    w_windows = field_in.shape[2] // WW
    feature_count = field_in.shape[3]
    blocked = field_in.reshape(
        z_windows, WZ, h_windows, WH, w_windows, WW, feature_count
    ).transpose(0, 2, 4, 1, 3, 5, 6)
    return blocked.reshape(z_windows * h_windows * w_windows, WZ * WH * WW, feature_count)


def from_windows(blocks, level_cells, row_cells, col_cells):
    feature_count = blocks.shape[-1]
    blocked = blocks.reshape(
        level_cells // WZ, row_cells // WH, col_cells // WW, WZ, WH, WW, feature_count
    ).transpose(0, 3, 1, 4, 2, 5, 6)
    return blocked.reshape(level_cells, row_cells, col_cells, feature_count)


def into_frame(payload, marker):
    payload = jnp.roll(payload, -(WZ // 2), axis=0)
    marker = jnp.roll(marker, -(WZ // 2), axis=0)
    col_cut = WW // 2
    payload_in, marker_in = passed_along(
        (payload[:, :, :col_cut], marker[:, :, :col_cut]), "lon", -1
    )
    payload = jnp.concatenate([payload[:, :, col_cut:], payload_in], axis=2)
    marker = jnp.concatenate([marker[:, :, col_cut:], marker_in], axis=2)
    row_cut = WH // 2
    payload_in, marker_in = passed_along((payload[:, :row_cut], marker[:, :row_cut]), "lat", -1)
    return (
        jnp.concatenate([payload[:, row_cut:], payload_in], axis=1),
        jnp.concatenate([marker[:, row_cut:], marker_in], axis=1),
    )


def into_frame_grad(payload):
    payload = jnp.roll(payload, -(WZ // 2), axis=0)
    col_cut = WW // 2
    payload_in = passed_along(payload[:, :, :col_cut], "lon", -1)
    payload = jnp.concatenate([payload[:, :, col_cut:], payload_in], axis=2)
    row_cut = WH // 2
    payload_in = passed_along(payload[:, :row_cut], "lat", -1)
    return jnp.concatenate([payload[:, row_cut:], payload_in], axis=1)


def out_of_frame(payload):
    row_cut = WH // 2
    payload_in = passed_along(payload[:, -row_cut:], "lat", 1)
    payload = jnp.concatenate([payload_in, payload[:, :-row_cut]], axis=1)
    col_cut = WW // 2
    payload_in = passed_along(payload[:, :, -col_cut:], "lon", 1)
    payload = jnp.concatenate([payload_in, payload[:, :, :-col_cut]], axis=2)
    return jnp.roll(payload, WZ // 2, axis=0)


def out_of_frame_wide(payload):
    row_cut = WH // 2
    payload_in = passed_along(payload[:, -row_cut:].astype(jnp.bfloat16), "lat", 1).astype(
        jnp.float32
    )
    payload = jnp.concatenate([payload_in, payload[:, :-row_cut]], axis=1)
    col_cut = WW // 2
    payload_in = passed_along(shortened(payload[:, :, -col_cut:]), "lon", 1)
    payload = jnp.concatenate([payload_in, payload[:, :, :-col_cut]], axis=2)
    return jnp.roll(payload, WZ // 2, axis=0)


def attend(activation, labels, bias_rows, w_qkv):
    window_count, window_cells, channels = activation.shape
    head_dim = channels // HEADS
    qkv_rows = (
        flat_dot(activation, w_qkv)
        .astype(jnp.bfloat16)
        .reshape(window_count, window_cells, 3, HEADS, head_dim)
    )
    queries = qkv_rows[:, :, 0]
    key_rows = qkv_rows[:, :, 1]
    values = qkv_rows[:, :, 2]
    scores = batched("nqhd,nkhd->nhqk", queries, key_rows) * head_dim ** (-0.5) + window_bias(
        bias_rows
    )
    allowed = labels[:, None, :, None] == labels[:, None, None, :]
    scores = jnp.where(allowed, scores, MASKED_SCORE)
    peak_val = jnp.max(scores, axis=-1, keepdims=True)
    raised = jnp.exp(scores - peak_val)
    attn_prob = raised / jnp.sum(raised, axis=-1, keepdims=True)
    prob_b = attn_prob.astype(jnp.bfloat16)
    mixed = (
        batched("nhqk,nkhd->nqhd", prob_b, values)
        .astype(jnp.bfloat16)
        .reshape(window_count, window_cells, channels)
    )
    return (mixed, (queries, key_rows, values, attn_prob, prob_b))


def attend_back(dmixed, saved, w_qkv):
    queries, key_rows, values, attn_prob, prob_b = saved
    window_count, window_cells, heads_here, head_dim = queries.shape
    dmixed = dmixed.reshape(window_count, window_cells, heads_here, head_dim)
    prob_grad = batched("nqhd,nkhd->nhqk", dmixed, values)
    value_grad = batched("nhqk,nqhd->nkhd", prob_b, dmixed)
    dscore = attn_prob * (prob_grad - jnp.sum(attn_prob * prob_grad, axis=-1, keepdims=True))
    row_grads = bias_grad(dscore)
    dscore_b = dscore.astype(jnp.bfloat16)
    scale_now = head_dim ** (-0.5)
    query_grad = batched("nhqk,nkhd->nqhd", dscore_b, key_rows) * scale_now
    key_grad = batched("nhqk,nqhd->nkhd", dscore_b, queries) * scale_now
    qkv_grads = jnp.stack([query_grad, key_grad, value_grad], axis=2).astype(jnp.bfloat16)
    qkv_grads = qkv_grads.reshape(window_count, window_cells, 3 * heads_here * head_dim)
    act_grads = flat_dot(qkv_grads, w_qkv.T)
    return (qkv_grads, act_grads, row_grads)


def middle(wide_in, mixed, gmask, w_proj, w_up, w_down):
    state_mid = (wide_in + flat_dot(mixed, w_proj)).astype(jnp.bfloat16)
    normed, inv_std = layer_norm(state_mid.astype(jnp.float32))
    normed_b = normed.astype(jnp.bfloat16)
    pre_act = flat_dot(normed_b, w_up)
    hidden = gelu_exact(pre_act).astype(jnp.bfloat16)
    down_part = grad_dot(hidden, gmask)
    hidden_grad = flat_dot(gmask, w_down.T)
    pre_grad = (hidden_grad * gelu_slope(pre_act)).astype(jnp.bfloat16)
    up_part = grad_dot(normed_b, pre_grad)
    normed_grad = flat_dot(pre_grad, w_up.T)
    dstate = (gmask.astype(jnp.float32) + norm_back(normed_grad, normed, inv_std)).astype(
        jnp.bfloat16
    )
    proj_part = grad_dot(mixed, dstate)
    dmixed = flat_dot(dstate, w_proj.T).astype(jnp.bfloat16)
    return (dstate, dmixed, proj_part, up_part, down_part)


def per_device(state_in, cotangent, w_qkv, w_proj, w_up, w_down, bias_table, pad_valid):
    lat_count = lax.axis_size("lat")
    lon_count = lax.axis_size("lon")
    channels = w_qkv.shape[0]
    levels, rows_dev, packed = state_in.shape
    cols_dev = packed // channels
    cells_in = state_in.reshape(levels, rows_dev, cols_dev, channels)
    grad_cells = cotangent.reshape(levels, rows_dev, cols_dev, channels)
    valid_mark = jnp.broadcast_to(
        pad_valid.astype(jnp.bfloat16)[None, None, :, None], (levels, rows_dev, cols_dev, 1)
    )
    lat_band = lax.axis_index("lat")
    level_tag = (jnp.arange(levels) >= levels - WZ // 2).astype(jnp.int32)
    row_tag = ((jnp.arange(rows_dev) >= rows_dev - WH // 2) & (lat_band == lat_count - 1)).astype(
        jnp.int32
    )
    type_count = bias_table.shape[0]
    level_windows = levels // WZ
    row_windows = rows_dev // WH
    type_grid = (
        jnp.arange(row_windows)[None, :, None] * level_windows
        + jnp.arange(level_windows)[:, None, None]
    )
    local_ids = type_grid.reshape(-1)
    bias_rows = jnp.take(bias_table, local_ids, axis=0)
    one_hot = (local_ids[:, None] == jnp.arange(type_count)[None, :]).astype(jnp.float32)
    wide_in = cells_in.astype(jnp.float32)
    normed, inv_std = layer_norm(wide_in)
    activation = normed.astype(jnp.bfloat16)
    shifted_act, marker = into_frame(activation, valid_mark)
    act_windows = to_windows(shifted_act)
    tagged = (
        level_tag[:, None, None] * 4
        + row_tag[None, :, None] * 2
        + (marker[..., 0] > 0.5).astype(jnp.int32)
    )
    mixed_windows, saved = attend(
        act_windows, to_windows(tagged[..., None])[..., 0], bias_rows, w_qkv
    )
    mixed = out_of_frame(from_windows(mixed_windows, levels, rows_dev, cols_dev))
    gmask = grad_cells * valid_mark
    dstate, dmixed, proj_part, up_part, down_part = middle(
        wide_in, mixed, gmask, w_proj, w_up, w_down
    )
    qkv_grads, act_grads, row_grads = attend_back(to_windows(into_frame_grad(dmixed)), saved, w_qkv)
    act_home = out_of_frame_wide(from_windows(act_grads, levels, rows_dev, cols_dev))
    input_grad = (dstate.astype(jnp.float32) + norm_back(act_home, normed, inv_std)).astype(
        jnp.bfloat16
    )
    qkv_part = grad_dot(act_windows, qkv_grads)
    table_grad = lax.psum(jnp.dot(one_hot.T, row_grads, precision=lax.Precision.HIGHEST), "lon")
    qkv_part, proj_part, up_part, down_part = lax.psum(
        (qkv_part, proj_part, up_part, down_part), ("lon", "lat")
    )
    factor = float(levels * rows_dev * cols_dev * lat_count * lon_count) ** (-0.5)
    return (
        input_grad.reshape(levels, rows_dev, packed),
        qkv_part * factor,
        proj_part * factor,
        up_part * factor,
        down_part * factor,
        table_grad,
    )


def solution(mesh):
    return jax.shard_map(
        per_device,
        mesh=mesh,
        in_specs=(
            P(None, "lat", "lon"),
            P(None, "lat", "lon"),
            P(),
            P(),
            P(),
            P(),
            P("lat", None),
            P("lon"),
        ),
        out_specs=(P(None, "lat", "lon"), P(), P(), P(), P(), P("lat", None)),
        check_vma=False,
    )
```

profile of v0, /device:TPU:1, one launch (start us, length us, event | category | flops | bytes accessed | tf_op | source)
XLA Modules:
  0.0 1052.4 jit_solution(6307301232746053845)
XLA Ops:
  8.0 8.8 collective-permute-start.2
  19.9 6.4 collective-permute-start
  27.0 1.4 gather_fusion
  28.4 2.3 gather.7
  31.3 1.6 reshape.304
  33.0 3.9 broadcast_and_fusion
  36.8 8.6 and.99
  45.5 3.1 fusion.69
  48.6 6.8 collective-permute-start.3
  55.7 2.9 reshape.305
  58.6 5.6 copy.90
  65.4 2.9 collective-permute-start.1
  69.1 5.1 collective-permute-done.1
  75.5 3.2 add_select_fusion
  78.8 1.8 copy-done.5
  80.5 2.4 fusion.67
  83.0 4.0 fusion.20
  88.4 1.9 collective-permute-start.4
  90.4 8.1 collective-permute-done.4
  98.6 1.9 collective-permute-start.5
  107.3 1.5 convolution_bitcast_fusion.2
  110.5 8.0 collective-permute-start.6
  118.5 1.6 convolution_bitcast_fusion.1
  120.3 2.6 collective-permute-start.7
  123.9 4.2 collective-permute-done.7
  128.8 1.3 copy.102
  130.1 5.0 convolution_bitcast_fusion
  135.1 2.0 multiply_reduce_fusion
  138.7 1.4 fusion.16
  141.3 3.4 copy.114
  144.7 1.5 maximum_convert_fusion
  147.3 2.1 copy.113
  149.3 4.5 copy.107
  153.8 3.4 reshape.326
  157.2 2.4 convert_element_type.127
  159.7 4.2 convert_element_type.123
  165.1 1.9 collective-permute-start.8
  168.6 13.6 %fusion.11 = f32[4,6,2,2,6,6,23]{6,4,5,3,2,1,0:T(8,128)S(1)} fusion(f32[4,6,2,6,1728,1,1]{4,3,2,1,0,5,6:T(8,128)} %reshape.326, pred[23,1728]{1,0:T(8,128)(4,1)S(1)} %copy-done.27, pred[2,6,1728]{2,1,0:T(8,128)(4,1)S(1)} %copy-done.28), kind=kOutput, calls=%fused_computation.23 | convolution fusion | flops 1648740096 | bytes 2369088 | tf_op jit(solution)/shard_map/dot_general | solution.py:101
  182.8 1.7 reshape.307
  185.6 2.1 collective-permute-start.9
  187.6 2.2 fusion.60
  189.8 2.2 collective-permute-done.9
  194.4 448.7 %all-reduce.6.cloned.1.call-done = (f32[192,576]{1,0:T(8,128)}, f32[192,192]{1,0:T(8,128)}, f32[192,768]{1,0:T(8,128)}, f32[768,192]{0,1:T(8,128)}) async-done(((f32[192,576]{1,0:T(8,128)}, f32[192,192]{1,0:T(8,128)}, f32[192,768]{1,0:T(8,128)}, f32[768,192]{0,1:T(8,128)}), (f32[192,576]{1,0:T(8,128)}, f32[192,192]{1,0:T(8,128)}, f32[192,768]{1,0:T(8,128)}, ...) | async-done | bytes 1769488 | tf_op jit(solution)/shard_map/psum | solution.py:290
  643.0 1.9 broadcast_multiply_fusion.2
  645.0 1.9 broadcast_multiply_fusion.1
  646.9 1.6 broadcast_multiply_fusion.3
  649.4 394.2 %all-reduce.4.cloned.1.call-done = f32[4,19872]{1,0:T(4,128)} async-done(((f32[4,19872]{1,0:T(4,128)}), f32[4,19872]{1,0:T(4,128)}) %all-reduce.4.cloned.1.call-update) | async-done | bytes 317968 | tf_op jit(solution)/shard_map/psum | solution.py:289
  1043.6 1.7 copy.173
  (163 shorter events, 31.4 us)
Async XLA Ops:
  7.2 19.8 %copy-start = (f32[4,19872]{1,0:T(4,128)S(1)}, f32[4,19872]{1,0:T(4,128)}, u32[]{:S(2)}) copy-start(f32[4,19872]{1,0:T(4,128)} %param.14) | copy-start | bytes 953860
  7.2 635.9 %all-reduce.6.cloned.1.call-start = ((), (), s32[]{:S(2)}) async-start(), calls=%async_computation.1 | async-start | bytes 3735552 | tf_op jit(solution)/shard_map/psum | solution.py:290
  8.0 40.5 %collective-permute-start.2 = (bf16[8,6,6,1]{2,1,0,3:T(8,128)(2,1)S(1)}, bf16[8,6,6,1]{2,1,0,3:T(8,128)(2,1)S(1)}, u32[]{:S(2)}, u32[]{:S(2)}) collective-permute-start(bf16[8,6,6,1]{2,1,0,3:T(8,128)(2,1)S(1)} %get-tuple-element.33), channel_id=1, source_target_pairs={{0,504},{8,0},{16,8},{24,16},{32,24},{40,32},{48,40},{56,48},{64,5... | collective-permute-start | bytes 1736 | tf_op jit(solution)/shard_map/ppermute | solution.py:19
  18.1 86.5 %copy-start.2 = (f32[8,6,12,192]{3,2,0,1:T(8,128)}, f32[8,6,12,192]{3,2,0,1:T(8,128)S(1)}, u32[]{:S(2)}) copy-start(f32[8,6,12,192]{3,2,0,1:T(8,128)S(1)} %reshape.308) | copy-start | bytes 1327108
  18.3 1.6 copy-start.17
  18.7 1.2 copy-start.21
  19.9 44.4 %collective-permute-start = (bf16[8,6,6,192]{3,2,1,0:T(8,128)(2,1)}, bf16[8,6,6,192]{3,2,1,0:T(8,128)(2,1)}, u32[]{:S(2)}, u32[]{:S(2)}) collective-permute-start(bf16[8,6,6,192]{3,2,1,0:T(8,128)(2,1)} %get-tuple-element.29), channel_id=1, source_target_pairs={{0,504},{8,0},{16,8},{24,16},{32,24},{40,32},{48,40},{56,48},{64,5... | collective-permute-start | bytes 331784 | tf_op jit(solution)/shard_map/ppermute | solution.py:19
  31.2 1.6 copy-start.29
  48.6 15.5 %collective-permute-start.3 = (bf16[8,3,12,1]{2,1,0,3:T(4,128)(2,1)S(1)}, bf16[8,3,12,1]{2,1,0,3:T(4,128)(2,1)S(1)}, u32[]{:S(2)}, u32[]{:S(2)}) collective-permute-start(bf16[8,3,12,1]{2,1,0,3:T(4,128)(2,1)S(1)} %get-tuple-element.31), channel_id=1, source_target_pairs={{0,7},{1,0},{2,1},{3,2},{4,3},{5,4},{6,5},{7,6},{8,15},{9,8},{10,9... | collective-permute-start | bytes 1736 | tf_op jit(solution)/shard_map/ppermute | solution.py:19
  58.6 5.7 copy-start.19
  64.2 10.3 copy-start.15
  65.4 8.8 collective-permute-start.1
  75.5 7.5 copy-start.9
  78.7 1.8 copy-start.5
  83.0 4.1 copy-start.24
  87.7 15.6 %copy-start.23 = (bf16[8,6,2304]{2,0,1:T(8,128)(2,1)S(1)}, bf16[8,6,2304]{2,0,1:T(8,128)(2,1)}, u32[]{:S(2)}) copy-start(bf16[8,6,2304]{2,0,1:T(8,128)(2,1)} %param.9) | copy-start | bytes 663556
  88.4 16.2 %copy-start.26 = (bf16[192,192]{1,0:T(8,128)(2,1)S(1)}, bf16[192,192]{1,0:T(8,128)(2,1)}, u32[]{:S(2)}) copy-start(bf16[192,192]{1,0:T(8,128)(2,1)} %param.11) | copy-start | bytes 221188
  88.4 10.0 collective-permute-start.4
  98.6 6.0 collective-permute-start.5
  103.7 1.7 copy-start.13
  104.9 1.0 copy-start.30
  110.0 12.8 %copy-start.11 = (bf16[8,6,12,192]{3,2,1,0:T(8,128)(2,1)}, bf16[8,6,12,192]{3,2,1,0:T(8,128)(2,1)S(1)}, u32[]{:S(2)}) copy-start(bf16[8,6,12,192]{3,2,1,0:T(8,128)(2,1)S(1)} %add_convert_fusion.1) | copy-start | bytes 663556
  110.5 9.6 collective-permute-start.6
  120.3 7.9 collective-permute-start.7
  130.1 5.0 copy-start.6
  135.1 2.3 copy-start.7
  135.1 2.3 copy-start.25
  137.4 1.3 copy-start.10
  146.2 1.1 copy-start.8
  149.3 4.5 copy-start.4
  159.6 4.3 copy-start.16
  159.7 7.4 copy-start.14
  164.4 4.2 copy-start.27
  164.4 4.2 copy-start.28
  165.1 19.4 %collective-permute-start.8 = (bf16[8,3,12,192]{3,2,1,0:T(8,128)(2,1)}, bf16[8,3,12,192]{3,2,1,0:T(8,128)(2,1)}, u32[]{:S(2)}, u32[]{:S(2)}) collective-permute-start(bf16[8,3,12,192]{3,2,1,0:T(8,128)(2,1)} %slice.227), channel_id=1, source_target_pairs={{0,1},{1,2},{2,3},{3,4},{4,5},{5,6},{6,7},{7,0},{8,9},{9,10},{10,1... | collective-permute-start | bytes 331784 | tf_op jit(solution)/shard_map/ppermute | solution.py:19
  168.3 875.3 %all-reduce.4.cloned.1.call-start = ((), (), s32[]{:S(2)}) async-start(), calls=%async_computation | async-start | bytes 638976 | tf_op jit(solution)/shard_map/psum | solution.py:289
  182.8 9.3 copy-start.3
  184.5 7.6 copy-start.18
  184.5 7.6 copy-start.22
  185.5 7.3 copy-start.12
  185.6 6.5 collective-permute-start.9
  193.3 852.1 %copy-start.1 = (f32[4,19872]{1,0:T(4,128)S(1)}, f32[4,19872]{1,0:T(4,128)}, u32[]{:S(2)}) copy-start(f32[4,19872]{1,0:T(4,128)} %param.14) | copy-start | bytes 953860
  643.0 5.5 copy-start.20
Sparse Core Ops, SparseCore 0:
  168.4 474.5 all-reduce.5
  646.0 397.5 all-reduce.3
where the time goes:
time: 1060 us; the launch traced here: 1050 us
  waiting for transfers between devices  863 us (81%)
  local copies, waits for them, and re-layouts  61.6 us (6%)
  matrix products  45.3 us (4%)
  starting transfers between devices  43.6 us (4%)
  other arithmetic  24.1 us (2%)
  between operations  15.2 us (1%)
    psum x1, waiting for transfers between devices, per_device(): lax.psum((qkv_part, proj_part, up_part, down_part), ('lon', 'lat'))  449 us
    psum x1, waiting for transfers between devices, per_device(): lax.psum(jnp.dot(one_hot.T, row_grads, precision=lax.Precision.HIGHEST),...  394 us
    ppermute x10, starting transfers between devices, passed_along(): return lax.ppermute(value, axis, pairs)  43.3 us
  transfers between devices with their start and end apart: 12, of which 6 were waited for; matrix products, arithmetic and copies ran while one was open for 7% of the time, Pallas kernels for 0%

commit v1 on v0

v1 whole, which is shorter than its diff:
```python
import functools

import jax
import jax.numpy as jnp
import numpy as np
from jax import lax
from jax.experimental import pallas as pl
from jax.experimental.pallas import tpu as pltpu
from jax.sharding import PartitionSpec as P

F32 = jnp.float32
BF16 = jnp.bfloat16
MESH = pl.DeviceIdType.MESH

C = 192
HEADS = 6
HEAD_DIM = 32
MLP = 768
WZ = 2
WH = 6
WW = 12
LEVELS = 8
WIN = WZ * WH * WW
NWIN = LEVELS // WZ
CELLS = WIN * NWIN
CH = WW // 2
RH = WH // 2
SLAB = LEVELS * RH
QUARTER = CH * SLAB
PACK = 2 * C
EXTRA = 16
SPAN = 2 * WW - 1
ZR = WZ * WH
TROWS = NWIN * HEADS * ZR
TCOLS = ZR * SPAN
TSEG = WH * SPAN
WCOLS = 3 * C + C + 2 * MLP
WTILES = (C // 16) * (WCOLS // 128)
TLANES = -(-TCOLS // 128)
TTILES = (TROWS // 16) * TLANES
XL = 2
NORM_EPS = 1e-5
MASKED = -1e30
VMEM_LIMIT = 56 * 1024 * 1024


def up_to(value, unit):
    return -(-value // unit) * unit


class Plan:
    def __init__(self, lon, lat):
        self.lon, self.lat = lon, lat
        self.nz = lon // (2 * XL)
        self.plane = XL * lat
        self.wt = -(-WTILES // (2 * self.plane))
        self.tt = -(-TTILES // (2 * XL))
        self.wrows = self.wt * 16 // self.nz
        self.trows = self.tt * 16 // self.nz
        self.toff = up_to(self.wrows, 8)
        self.zrows = up_to(self.toff + self.trows, 16)
        assert self.wrows * self.nz == self.wt * 16
        assert self.trows * self.nz == self.tt * 16


def cell_order():
    perm = np.zeros((CELLS, CELLS), np.float32)
    for w in range(NWIN):
        for c in range(WW):
            for z in range(WZ):
                for r in range(WH):
                    row = w * WIN + c * ZR + z * WH + r
                    quarter = (r // RH) * 2 + c // CH
                    col = quarter * QUARTER + (c % CH) * SLAB + w * WZ * RH + z * RH + r % RH
                    perm[row, col] = 1
    return perm


def slab_order():
    perm = np.zeros((2 * SLAB, LEVELS * 8), np.float32)
    for rs in range(2):
        for w in range(NWIN):
            for z in range(WZ):
                for r in range(RH):
                    row = rs * SLAB + w * WZ * RH + z * RH + r
                    perm[row, ((2 * w + z + WZ // 2) % LEVELS) * 8 + rs * RH + r] = 1
    return perm


def table_rows():
    perm = np.zeros((TROWS, TROWS), np.float32)
    for t in range(NWIN):
        for s in range(HEADS * ZR):
            perm[t * HEADS * ZR + s, s * NWIN + t] = 1
    return perm


def table_lanes():
    perm = np.zeros((TCOLS, TCOLS), np.float32)
    for b in range(ZR):
        for d in range(SPAN):
            perm[b * SPAN + d, (SPAN - 1 - d) * ZR + b] = 1
    return perm


def table_sums():
    hit = np.zeros((WW, WIN, TCOLS), np.float32)
    for ci in range(WW):
        for cj in range(WW):
            for b in range(ZR):
                hit[ci, cj * ZR + b, b * SPAN + ci - cj + WW - 1] = 1
    return hit


def column_of_cell():
    hit = np.zeros((WIN, EXTRA), np.float32)
    for c in range(WW):
        hit[c * ZR : (c + 1) * ZR, c] = 1
    return hit


def dot(a, b):
    return lax.dot_general(a, b, (((1,), (0,)), ((), ())), preferred_element_type=F32)


def dot_nt(a, b):
    return lax.dot_general(a, b, (((1,), (1,)), ((), ())), preferred_element_type=F32)


def dot_tn(a, b):
    return lax.dot_general(a, b, (((0,), (0,)), ((), ())), preferred_element_type=F32)


def neighbours(plan):
    lon, lat = lax.axis_index("lon"), lax.axis_index("lat")
    lon_b, lon_a = lax.rem(lon + plan.lon - 1, plan.lon), lax.rem(lon + 1, plan.lon)
    lat_b, lat_a = lax.rem(lat + plan.lat - 1, plan.lat), lax.rem(lat + 1, plan.lat)
    before = [(lon_b, lat), (lon, lat_b), (lon_b, lat_b)]
    after = [(lon_a, lat), (lon, lat_a), (lon_a, lat_a)]
    return before, after


def remote(src, dst, send, recv, place):
    return pltpu.make_async_remote_copy(
        src_ref=src, dst_ref=dst, send_sem=send, recv_sem=recv,
        device_id={"lon": place[0], "lat": place[1]}, device_id_type=MESH,
    )


def greet(place):
    pl.semaphore_signal(
        pltpu.get_barrier_semaphore(), inc=1,
        device_id={"lon": place[0], "lat": place[1]}, device_id_type=MESH,
    )


def enter_kernel(plan, x_ref, g_ref, valid_ref, slab_ref, out_ref, home, packed, send, recv, ssem, rsem):
    before, after = neighbours(plan)
    for place in before + after:
        greet(place)
    slab = slab_ref[...]
    packed[...] = jnp.zeros_like(packed)
    for part, ref in enumerate((x_ref, g_ref)):
        home[...] = jnp.zeros_like(home)
        for level in range(LEVELS):
            home[8 * level : 8 * level + WH, :] = ref[level].astype(F32)
        rows = dot(slab, home[...].astype(BF16))
        for c in range(WW):
            for rs in range(2):
                piece = rows[rs * SLAB : (rs + 1) * SLAB, c * C : (c + 1) * C]
                if part == 1:
                    piece = piece * valid_ref[0, c].astype(F32)
                packed[
                    rs * 2 + c // CH, (c % CH) * SLAB : (c % CH + 1) * SLAB, part * C : (part + 1) * C
                ] = piece
    for c in range(WW):
        mark = jnp.full((1, PACK), valid_ref[0, c].astype(F32), F32)
        for rs in range(2):
            packed[rs * 2 + c // CH, QUARTER + c % CH : QUARTER + c % CH + 1, :] = mark
    send[...] = packed[...].astype(BF16)
    pl.semaphore_wait(pltpu.get_barrier_semaphore(), 6)
    copies = [
        remote(send.at[2], recv.at[1], ssem.at[0], rsem.at[0], before[0]),
        remote(send.at[1], recv.at[2], ssem.at[1], rsem.at[1], before[1]),
        remote(send.at[0], recv.at[3], ssem.at[2], rsem.at[2], before[2]),
    ]
    for copy in copies:
        copy.start()
    out_ref[0] = send[3]
    for copy in copies:
        copy.wait()
    for q in range(1, 4):
        out_ref[q] = recv[q]


def enter_frame(plan, state, cotangent, valid):
    shape = (4, QUARTER + EXTRA, PACK)
    vmem = pl.BlockSpec(memory_space=pltpu.VMEM)
    return pl.pallas_call(
        functools.partial(enter_kernel, plan),
        out_shape=jax.ShapeDtypeStruct(shape, BF16),
        in_specs=[vmem, vmem, pl.BlockSpec(memory_space=pltpu.SMEM), vmem],
        out_specs=vmem,
        scratch_shapes=[
            pltpu.VMEM((LEVELS * 8, WW * C), F32),
            pltpu.VMEM(shape, F32),
            pltpu.VMEM(shape, BF16),
            pltpu.VMEM(shape, BF16),
            pltpu.SemaphoreType.DMA((3,)),
            pltpu.SemaphoreType.DMA((3,)),
        ],
        compiler_params=pltpu.CompilerParams(
            collective_id=0, has_side_effects=True, vmem_limit_bytes=VMEM_LIMIT
        ),
        name="enter_frame",
    )(state, cotangent, valid.reshape(1, WW), jnp.asarray(slab_order(), BF16))


def normed_of(v):
    centred = v - jnp.mean(v, axis=-1, keepdims=True)
    inv = lax.rsqrt(jnp.mean(centred * centred, axis=-1, keepdims=True) + NORM_EPS)
    return centred * inv, inv


def norm_back(up, normed, inv):
    return inv * (
        up
        - jnp.mean(up, axis=-1, keepdims=True)
        - normed * jnp.mean(up * normed, axis=-1, keepdims=True)
    )


def block_kernel(
    plan,
    frame_ref, w_qkv, w_proj, w_up, w_down, table_ref,
    order_ref, back_ref, trow_ref, tlane_ref, tsum_ref, ccol_ref,
    dx_ref, wout_ref, tout_ref,
    xs, gm, act, act_inv, q_s, k_s, v_s, o_s, dh_s, dout_s, b_s, m_s, du_s, dqkv_s,
    tn, bias, prob, dcol, total, tgrad,
):
    hm = []
    lane = lax.broadcasted_iota(jnp.int32, (1, C), 1)
    for h in range(HEADS):
        hm.append(jnp.where(lane // HEAD_DIM == h, 1.0, 0.0).astype(BF16))
    scale = HEAD_DIM ** (-0.5)

    quarters = frame_ref[:, :QUARTER, :].reshape(CELLS, PACK)
    cells = dot(order_ref[...], quarters)
    xs[...] = cells[:, :C]
    gm[...] = cells[:, C:].astype(BF16)

    for h in range(HEADS):
        for zi in range(WZ):
            for zj in range(WZ):
                for ri in range(WH):
                    seg = ((h * WZ + zi) * WZ + zj) * WH + ri
                    row = (h * ZR + zi * WH + ri) * NWIN
                    tn[row : row + NWIN, zj * TSEG : (zj + 1) * TSEG] = table_ref[
                        :, seg * TSEG : (seg + 1) * TSEG
                    ]
    left = tn[...]
    spread = jnp.zeros((TROWS, TCOLS), F32)
    for _ in range(3):
        term = left.astype(BF16)
        left = left - term.astype(F32)
        spread += dot(dot(trow_ref[...], term).astype(BF16), tlane_ref[...])
    tn[...] = spread

    marks = jnp.concatenate(
        [
            frame_ref[0, QUARTER : QUARTER + EXTRA, :WIN][:CH].astype(F32),
            frame_ref[1, QUARTER : QUARTER + EXTRA, :WIN][:CH].astype(F32),
            jnp.zeros((EXTRA - WW, WIN), F32),
        ],
        axis=0,
    ).astype(BF16)
    ccol = ccol_ref[...]
    same = dot(ccol, marks) == lax.dot_general(
        marks, ccol, (((0,), (1,)), ((), ())), preferred_element_type=F32
    )
    ii = lax.broadcasted_iota(jnp.int32, (WIN, WIN), 0)
    jj = lax.broadcasted_iota(jnp.int32, (WIN, WIN), 1)
    low_i, low_j = (lax.rem(ii, WH) >= RH).astype(jnp.int32), (lax.rem(jj, WH) >= RH).astype(jnp.int32)
    seam = lax.axis_index("lat") == plan.lat - 1
    open_rows = jnp.where(seam, 0, 1)
    same = same & ((low_i == low_j) | (open_rows == 1))
    top_i, top_j = lax.rem(ii // WH, WZ), lax.rem(jj // WH, WZ)
    barred = jnp.where(same, 0.0, MASKED)
    barred_top = jnp.where(top_i == top_j, barred, MASKED)

    for t in range(NWIN):
        bar = barred_top if t == NWIN - 1 else barred
        for ci in range(WW):
            rows = tn[t * HEADS * ZR : (t + 1) * HEADS * ZR, (WW - 1 - ci) * ZR : (WW - 1 - ci) * ZR + WIN]
            for h in range(HEADS):
                bias[t * HEADS + h, ci * ZR : (ci + 1) * ZR, :] = (
                    rows[h * ZR : (h + 1) * ZR, :] + bar[ci * ZR : (ci + 1) * ZR, :]
                )

    normed, inv = normed_of(xs[...])
    a = normed.astype(BF16)
    act[...] = a
    q_s[...] = dot(a, w_qkv[:, :C]).astype(BF16)
    k_s[...] = dot(a, w_qkv[:, C : 2 * C]).astype(BF16)
    v_s[...] = dot(a, w_qkv[:, 2 * C :]).astype(BF16)

    def forward(w, carry):
        at = pl.ds(pl.multiple_of(w * WIN, WIN), WIN)
        q, k, v = q_s[at, :], k_s[at, :], v_s[at, :]
        mixed = jnp.zeros((WIN, C), F32)
        for h in range(HEADS):
            s = dot_nt(q * hm[h], k) * scale + bias[w * HEADS + h]
            e = jnp.exp(s - jnp.max(s, axis=-1, keepdims=True))
            p = e * (1.0 / jnp.sum(e, axis=-1, keepdims=True))
            prob[w * HEADS + h] = p
            mixed += dot(p.astype(BF16), v * hm[h])
        o_s[at, :] = mixed.astype(BF16)
        return carry

    lax.fori_loop(0, NWIN, forward, 0)

    def middle(w, carry):
        at = pl.ds(pl.multiple_of(w * WIN, WIN), WIN)
        hs = (xs[at, :] + dot(o_s[at, :], w_proj[...])).astype(BF16).astype(F32)
        n2, inv2 = normed_of(hs)
        b = n2.astype(BF16)
        b_s[at, :] = b
        u = dot(b, w_up[...])
        cdf = 0.5 * (1.0 + lax.erf(u * 0.7071067811865476))
        m_s[at, :] = (u * cdf).astype(BF16)
        slope = cdf + u * jnp.exp(-0.5 * u * u) * 0.3989422804014327
        g = gm[at, :]
        du = (dot_nt(g, w_down[...]) * slope).astype(BF16)
        du_s[at, :] = du
        dh = (g.astype(F32) + norm_back(dot_nt(du, w_up[...]), n2, inv2)).astype(BF16)
        dh_s[at, :] = dh
        dout_s[at, :] = dot_nt(dh, w_proj[...]).astype(BF16)
        return carry

    lax.fori_loop(0, NWIN, middle, 0)
    total[:, 3 * C : 4 * C] = dot_tn(o_s[...], dh_s[...])
    total[:, 4 * C : 4 * C + MLP] = dot_tn(b_s[...], du_s[...])
    total[:, 4 * C + MLP :] = dot_tn(gm[...], m_s[...])

    for w in range(NWIN):
        at = pl.ds(w * WIN, WIN)
        q, k, v, do = q_s[at, :], k_s[at, :], v_s[at, :], dout_s[at, :]
        dq, dk, dv = (jnp.zeros((WIN, C), F32) for _ in range(3))
        for h in range(HEADS):
            p = prob[w * HEADS + h]
            do_h = do * hm[h]
            dp = dot_nt(do_h, v)
            ds = p * (dp - jnp.sum(p * dp, axis=-1, keepdims=True))
            first = (w * HEADS + h) * ZR
            for ci in range(WW):
                dcol[ci, first : first + ZR, :] = ds[ci * ZR : (ci + 1) * ZR, :]
            dsb = ds.astype(BF16)
            dq += dot(dsb, k * hm[h])
            dk += dot_tn(dsb, q * hm[h])
            dv += dot_tn(p.astype(BF16), do_h)
        dqkv_s[at, 0:C] = (dq * scale).astype(BF16)
        dqkv_s[at, C : 2 * C] = (dk * scale).astype(BF16)
        dqkv_s[at, 2 * C :] = dv.astype(BF16)

    dqkv = dqkv_s[...]
    total[:, : 3 * C] = dot_tn(act[...], dqkv)
    back = dot_nt(dqkv, w_qkv[...])
    normed, inv = normed_of(xs[...])
    dxs = (dh_s[...].astype(F32) + norm_back(back, normed, inv)).astype(BF16)
    dx_ref[...] = dot(back_ref[...], dxs).astype(BF16).reshape(4, QUARTER, C)

    grad = jnp.zeros((TROWS, TCOLS), F32)
    for ci in range(WW):
        grad += dot(dcol[ci].astype(BF16), tsum_ref[ci])
    tgrad[...] = jnp.zeros_like(tgrad)
    tgrad[:, :TCOLS] = dot_tn(trow_ref[...], grad.astype(BF16))
    tiles = TROWS // 16 * TLANES
    for i in range(4 * plan.tt):
        core, rest = divmod(i, XL * plan.tt)
        place = (core, rest // plan.tt, rest % plan.tt)
        if i < tiles:
            r, l = divmod(i, TLANES)
            tout_ref[place] = tgrad[r * 16 : r * 16 + 16, l * 128 : l * 128 + 128].astype(BF16)
        else:
            tout_ref[place] = jnp.zeros((16, 128), BF16)
    for i in range(2 * plan.plane * plan.wt):
        core, rest = divmod(i, plan.plane * plan.wt)
        place = (core, rest // plan.wt, rest % plan.wt)
        if i < WTILES:
            r, l = divmod(i, WCOLS // 128)
            wout_ref[place] = total[r * 16 : r * 16 + 16, l * 128 : l * 128 + 128].astype(BF16)
        else:
            wout_ref[place] = jnp.zeros((16, 128), BF16)


def block(plan, frame, w_qkv, w_proj, w_up, w_down, table):
    vmem = pl.BlockSpec(memory_space=pltpu.VMEM)
    order = cell_order()
    return pl.pallas_call(
        functools.partial(block_kernel, plan),
        out_shape=(
            jax.ShapeDtypeStruct((4, QUARTER, C), BF16),
            jax.ShapeDtypeStruct((2, plan.plane, plan.wt, 16, 128), BF16),
            jax.ShapeDtypeStruct((2, XL, plan.tt, 16, 128), BF16),
        ),
        in_specs=[vmem] * 12,
        out_specs=(vmem, vmem, vmem),
        scratch_shapes=[
            pltpu.VMEM((CELLS, C), F32),
            pltpu.VMEM((CELLS, C), BF16),
            pltpu.VMEM((CELLS, C), BF16),
            pltpu.VMEM((CELLS, 1), F32),
            pltpu.VMEM((CELLS, C), BF16),
            pltpu.VMEM((CELLS, C), BF16),
            pltpu.VMEM((CELLS, C), BF16),
            pltpu.VMEM((CELLS, C), BF16),
            pltpu.VMEM((CELLS, C), BF16),
            pltpu.VMEM((CELLS, C), BF16),
            pltpu.VMEM((CELLS, C), BF16),
            pltpu.VMEM((CELLS, MLP), BF16),
            pltpu.VMEM((CELLS, MLP), BF16),
            pltpu.VMEM((CELLS, 3 * C), BF16),
            pltpu.VMEM((TROWS, TCOLS), F32),
            pltpu.VMEM((NWIN * HEADS, WIN, WIN), F32),
            pltpu.VMEM((NWIN * HEADS, WIN, WIN), F32),
            pltpu.VMEM((WW, TROWS, WIN), F32),
            pltpu.VMEM((C, WCOLS), F32),
            pltpu.VMEM((TROWS, TLANES * 128), F32),
        ],
        compiler_params=pltpu.CompilerParams(vmem_limit_bytes=VMEM_LIMIT),
        name="block",
    )(
        frame, w_qkv, w_proj, w_up, w_down, table,
        jnp.asarray(order, BF16), jnp.asarray(order.T, BF16), jnp.asarray(table_rows(), BF16),
        jnp.asarray(table_lanes(), BF16), jnp.asarray(table_sums(), BF16),
        jnp.asarray(column_of_cell(), BF16),
    )


def share_kernel(
    plan, dx_ref, wsend, tsend, home_ref, wall_ref, tall_ref,
    hrecv, wr1, tr1, w1, t1, wr2, tr2, rows, zrows, zsend, zrecv, zall, wall, tall,
    hs, hr, c1s, c1r, p2s, p2r, t2s, t2r, z1s, z1r, z2s, z2r, p3s, p3r, t3s, t3r, c4s, c4r,
):
    lon, lat = lax.axis_index("lon"), lax.axis_index("lat")
    nz, plane = plan.nz, plan.plane
    core = lax.rem(lon, 2)
    z = lax.rem(lon // 2, nz)
    xl = lon // (2 * nz)
    me = xl * plan.lat + lat

    def at(p, zz, cc):
        return (p // plan.lat) * (2 * nz) + zz * 2 + cc, lax.rem(p, plan.lat)

    def plane_peer(d):
        return lax.rem(me + d, plane)

    def z_peer(d):
        return lax.rem(z + d, nz)

    def plane_from(d):
        return lax.rem(me - d + plane, plane)

    other = at(me, z, 1 - core)
    across = at((1 - xl) * plan.lat + lat, z, core)
    before, after = neighbours(plan)
    greet(other)
    for place in before + after:
        greet(place)

    def greet_plane(d, carry):
        greet(at(plane_peer(d), z, core))
        return carry

    def greet_z(d, carry):
        greet(at(me, z_peer(d), core))
        return carry

    lax.fori_loop(1, plane, greet_plane, 0)
    lax.fori_loop(1, nz, greet_z, 0)
    pl.semaphore_wait(pltpu.get_barrier_semaphore(), 7 + plane - 1 + nz - 1)

    first = [
        remote(wsend.at[1 - core], wr1, c1s.at[0], c1r.at[0], other),
        remote(tsend.at[1 - core], tr1, c1s.at[1], c1r.at[1], other),
    ]
    for copy in first:
        copy.start()
    home = [
        remote(dx_ref.at[1], hrecv.at[2], hs.at[0], hr.at[0], after[0]),
        remote(dx_ref.at[2], hrecv.at[1], hs.at[1], hr.at[1], after[1]),
        remote(dx_ref.at[3], hrecv.at[0], hs.at[2], hr.at[2], after[2]),
    ]
    for copy in home:
        copy.start()
    home_ref[3] = dx_ref[0]
    for copy in first:
        copy.wait_recv()

    def piece_out(d):
        p = plane_peer(d)
        return remote(w1.at[p], wr2.at[d], p2s.at[d], p2r.at[d], at(p, z, core))

    def send_piece(d, carry):
        p = plane_peer(d)
        w1[p] = (wsend[core, p].astype(F32) + wr1[p].astype(F32)).astype(BF16)
        piece_out(d).start()
        return carry

    lax.fori_loop(1, plane, send_piece, 0)
    t1[...] = (tsend[core, 1 - xl].astype(F32) + tr1[1 - xl].astype(F32)).astype(BF16)
    table_out = remote(t1, tr2, t2s.at[0], t2r.at[0], across)
    table_out.start()
    wsum = wsend[core, me].astype(F32) + wr1[me].astype(F32)
    tsum = tsend[core, xl].astype(F32) + tr1[xl].astype(F32)

    def take_piece(d, acc):
        piece_out(d).wait_recv()
        return acc + wr2[d].astype(F32)

    wsum = lax.fori_loop(1, plane, take_piece, wsum)
    table_out.wait_recv()
    tsum = tsum + tr2[...].astype(F32)

    wlen, tlen = plan.wt * 16, plan.tt * 16
    rows[:wlen, :] = wsum.reshape(wlen, 128)
    rows[wlen:, :] = tsum.reshape(tlen, 128)
    zrows[...] = jnp.zeros_like(zrows)
    wr, tr, to = plan.wrows, plan.trows, plan.toff
    for i in range(nz):
        zrows[i, :wr, :] = rows[i * wr : (i + 1) * wr, :]
        zrows[i, to : to + tr, :] = rows[wlen + i * tr : wlen + (i + 1) * tr, :]
    zsend[...] = zrows[...].astype(BF16)

    def z_out(d):
        p = z_peer(d)
        return remote(zsend.at[p], zrecv.at[d], z1s.at[d], z1r.at[d], at(me, p, core))

    def z_back(d):
        return remote(zall.at[z], zall.at[z], z2s.at[d], z2r.at[d], at(me, z_peer(d), core))

    def start_z_out(d, carry):
        z_out(d).start()
        return carry

    def take_z(d, acc):
        z_out(d).wait_recv()
        return acc + zrecv[d].astype(F32)

    def start_z_back(d, carry):
        z_back(d).start()
        return carry

    def wait_z_back(d, carry):
        z_back(d).wait_recv()
        return carry

    lax.fori_loop(1, nz, start_z_out, 0)
    zall[z] = lax.fori_loop(1, nz, take_z, zsend[z].astype(F32)).astype(BF16)
    lax.fori_loop(1, nz, start_z_back, 0)
    lax.fori_loop(1, nz, wait_z_back, 0)
    zrows[...] = zall[...].astype(F32)
    for i in range(nz):
        rows[i * wr : (i + 1) * wr, :] = zrows[i, :wr, :]
        rows[wlen + i * tr : wlen + (i + 1) * tr, :] = zrows[i, to : to + tr, :]
    wall[core, me] = rows[:wlen, :].astype(BF16).reshape(plan.wt, 16, 128)
    tall[core, xl] = rows[wlen:, :].astype(BF16).reshape(plan.tt, 16, 128)

    def sum_out(d):
        mine = wall.at[core, me]
        return remote(mine, mine, p3s.at[d], p3r.at[d], at(plane_peer(d), z, core))

    def hand_over(d):
        held = wall.at[core, plane_from(d)]
        return remote(held, held, c4s.at[d], c4r.at[d], other)

    def table_hand(i, owner):
        held = tall.at[core, owner]
        return remote(held, held, c4s.at[plane + i], c4r.at[plane + i], other)

    def start_sum_out(d, carry):
        sum_out(d).start()
        return carry

    def forward_sum(d, carry):
        sum_out(d).wait_recv()
        hand_over(d).start()
        return carry

    mine_t = tall.at[core, xl]
    table_back = remote(mine_t, mine_t, t3s.at[0], t3r.at[0], across)
    table_back.start()
    lax.fori_loop(1, plane, start_sum_out, 0)
    hand_over(0).start()
    table_hand(0, xl).start()
    table_back.wait_recv()
    table_hand(1, 1 - xl).start()
    lax.fori_loop(1, plane, forward_sum, 0)

    def wait_hand(d, carry):
        hand_over(d).wait_recv()
        return carry

    lax.fori_loop(0, plane, wait_hand, 0)
    table_hand(0, xl).wait_recv()
    table_hand(1, 1 - xl).wait_recv()
    for copy in home:
        copy.wait_recv()
    for q in range(3):
        home_ref[q] = hrecv[q]
    wall_ref[...] = wall[...]
    tall_ref[...] = tall[...]

    for copy in first + home + [table_out, table_back, table_hand(0, xl), table_hand(1, 1 - xl)]:
        copy.wait_send()

    def drain_plane(d, carry):
        piece_out(d).wait_send()
        sum_out(d).wait_send()
        return carry

    def drain_z(d, carry):
        z_out(d).wait_send()
        z_back(d).wait_send()
        return carry

    def drain_hand(d, carry):
        hand_over(d).wait_send()
        return carry

    lax.fori_loop(1, plane, drain_plane, 0)
    lax.fori_loop(1, nz, drain_z, 0)
    lax.fori_loop(0, plane, drain_hand, 0)


def share(plan, dx, wsend, tsend):
    vmem = pl.BlockSpec(memory_space=pltpu.VMEM)
    plane, nz = plan.plane, plan.nz
    sem = pltpu.SemaphoreType.DMA
    lines = (plan.wt + plan.tt) * 16
    return pl.pallas_call(
        functools.partial(share_kernel, plan),
        out_shape=(
            jax.ShapeDtypeStruct(dx.shape, BF16),
            jax.ShapeDtypeStruct(wsend.shape, BF16),
            jax.ShapeDtypeStruct(tsend.shape, BF16),
        ),
        in_specs=[vmem] * 3,
        out_specs=(vmem,) * 3,
        scratch_shapes=[
            pltpu.VMEM((3, QUARTER, C), BF16),
            pltpu.VMEM(wsend.shape[1:], BF16),
            pltpu.VMEM(tsend.shape[1:], BF16),
            pltpu.VMEM(wsend.shape[1:], BF16),
            pltpu.VMEM(tsend.shape[2:], BF16),
            pltpu.VMEM(wsend.shape[1:], BF16),
            pltpu.VMEM(tsend.shape[2:], BF16),
            pltpu.VMEM((lines, 128), F32),
            pltpu.VMEM((nz, plan.zrows, 128), F32),
            pltpu.VMEM((nz, plan.zrows, 128), BF16),
            pltpu.VMEM((nz, plan.zrows, 128), BF16),
            pltpu.VMEM((nz, plan.zrows, 128), BF16),
            pltpu.VMEM(wsend.shape, BF16),
            pltpu.VMEM(tsend.shape, BF16),
            sem((3,)), sem((3,)), sem((2,)), sem((2,)), sem((plane,)), sem((plane,)),
            sem((1,)), sem((1,)), sem((nz,)), sem((nz,)), sem((nz,)), sem((nz,)),
            sem((plane,)), sem((plane,)), sem((1,)), sem((1,)), sem((plane + 2,)), sem((plane + 2,)),
        ],
        compiler_params=pltpu.CompilerParams(
            collective_id=1, has_side_effects=True, vmem_limit_bytes=VMEM_LIMIT
        ),
        name="share",
    )(dx, wsend, tsend)


def write_kernel(
    plan, factor, home_ref, wall, tall, slab_ref,
    dx_ref, qkv_ref, proj_ref, up_ref, down_ref, table_ref, band, total, tgrad,
):
    for c in range(WW):
        for rs in range(2):
            band[rs * SLAB : (rs + 1) * SLAB, c * C : (c + 1) * C] = home_ref[
                rs * 2 + c // CH, (c % CH) * SLAB : (c % CH + 1) * SLAB, :
            ].astype(F32)
    rows = dot_tn(slab_ref[...], band[...].astype(BF16))
    for level in range(LEVELS):
        dx_ref[level] = rows[8 * level : 8 * level + WH, :].astype(BF16)
    for i in range(WTILES):
        core, rest = divmod(i, plan.plane * plan.wt)
        r, l = divmod(i, WCOLS // 128)
        total[r * 16 : r * 16 + 16, l * 128 : l * 128 + 128] = (
            wall[core, rest // plan.wt, rest % plan.wt].astype(F32) * factor
        )
    qkv_ref[...] = total[:, : 3 * C]
    proj_ref[...] = total[:, 3 * C : 4 * C]
    up_ref[...] = total[:, 4 * C : 4 * C + MLP]
    down_ref[...] = total[:, 4 * C + MLP :].T
    for i in range(TTILES):
        core, rest = divmod(i, XL * plan.tt)
        r, l = divmod(i, TLANES)
        tgrad[r * 16 : r * 16 + 16, l * 128 : l * 128 + 128] = tall[
            core, rest // plan.tt, rest % plan.tt
        ].astype(F32)
    for h in range(HEADS):
        for zi in range(WZ):
            for zj in range(WZ):
                for ri in range(WH):
                    seg = ((h * WZ + zi) * WZ + zj) * WH + ri
                    row = (h * ZR + zi * WH + ri) * NWIN
                    table_ref[:, seg * TSEG : (seg + 1) * TSEG] = tgrad[
                        row : row + NWIN, zj * TSEG : (zj + 1) * TSEG
                    ]


def write(plan, home, wall, tall):
    vmem = pl.BlockSpec(memory_space=pltpu.VMEM)
    factor = float(CELLS * plan.lon * plan.lat) ** (-0.5)
    return pl.pallas_call(
        functools.partial(write_kernel, plan, factor),
        out_shape=(
            jax.ShapeDtypeStruct((LEVELS, WH, WW * C), BF16),
            jax.ShapeDtypeStruct((C, 3 * C), F32),
            jax.ShapeDtypeStruct((C, C), F32),
            jax.ShapeDtypeStruct((C, MLP), F32),
            jax.ShapeDtypeStruct((MLP, C), F32),
            jax.ShapeDtypeStruct((NWIN, HEADS * ZR * ZR * SPAN), F32),
        ),
        in_specs=[vmem] * 4,
        out_specs=(vmem,) * 6,
        scratch_shapes=[
            pltpu.VMEM((2 * SLAB, WW * C), F32),
            pltpu.VMEM((C, WCOLS), F32),
            pltpu.VMEM((TROWS, TLANES * 128), F32),
        ],
        compiler_params=pltpu.CompilerParams(vmem_limit_bytes=VMEM_LIMIT),
        name="write",
    )(home, wall, tall, jnp.asarray(slab_order(), BF16))


def per_device(plan, state_in, cotangent, w_qkv, w_proj, w_up, w_down, bias_table, pad_valid):
    frame = enter_frame(plan, state_in, cotangent, pad_valid)
    dx, wsend, tsend = block(plan, frame, w_qkv, w_proj, w_up, w_down, bias_table)
    return write(plan, *share(plan, dx, wsend, tsend))


def solution(mesh):
    plan = Plan(mesh.shape["lon"], mesh.shape["lat"])
    return jax.shard_map(
        functools.partial(per_device, plan),
        mesh=mesh,
        in_specs=(
            P(None, "lat", "lon"),
            P(None, "lat", "lon"),
            P(),
            P(),
            P(),
            P(),
            P("lat", None),
            P("lon"),
        ),
        out_specs=(P(None, "lat", "lon"), P(), P(), P(), P(), P("lat", None)),
        check_vma=False,
    )
```

time: 1060 us -> 118 us (0.11)
  waiting for transfers between devices: 863 us -> 0 us
  Pallas kernels: 0 us -> 109 us
  local copies, waits for them, and re-layouts: 61.6 us -> 8.25 us
  matrix products: 45.3 us -> 0 us
  starting transfers between devices: 43.6 us -> 0 us
  other arithmetic: 24.1 us -> 0 us
  between operations: 15.2 us -> 0.67 us
    psum x2 -> x0, waiting for transfers between devices: 843 us -> none  [the longest x1 449 us: per_device(): lax.psum((qkv_part, proj_part, up_part, down_part), ('lon', 'lat'))]
    pallas_call x0 -> x4, Pallas kernels: none -> 109 us  [the longest x1 65.1 us: share(): pl.pallas_call(functools.partial(share_kernel, plan), out_shape=(jax.Shap...]
    dot_general x20 -> x0, matrix products: 45.3 us -> none  [the longest x6 16.9 us: batched(): jnp.einsum(formula, left_op, right_op, preferred_element_type=jnp.float32)]
    ppermute x10 -> x0, starting transfers between devices: 43.3 us -> none  [passed_along(): return lax.ppermute(value, axis, pairs)]
    ppermute x10 -> x0, waiting for transfers between devices: 19.7 us -> none  [passed_along(): return lax.ppermute(value, axis, pairs)]
    convert_element_type x8 -> x0, local copies, waits for them, and re-layouts: 15.8 us -> none  [the longest x4 13.2 us: attend_back(): jnp.stack([query_grad, key_grad, value_grad], axis=2).astype(jnp.bfloat16)]
    reshape x7 -> x0, local copies, waits for them, and re-layouts: 13.2 us -> none  [the longest x2 8.47 us: window_bias(): return spread.reshape(window_count, HEADS, window_cells, window_cells)]
    and x7 -> x0, local copies, waits for them, and re-layouts: 11.4 us -> none  [spread_table(): (row_level == col_level) & (row_lat == col_lat)]
  transfers between devices with their start and end apart: 12 -> 0, of which waited for: 6 -> 0; matrix products, arithmetic and copies ran while one was open for 7% -> 0% of each run, Pallas kernels for 0% -> 0%
where the time goes in v1:
time: 118 us
  Pallas kernels  109 us (92%)
  local copies, waits for them, and re-layouts  8.25 us (7%)
    pallas_call x1, Pallas kernels, share(): pl.pallas_call(functools.partial(share_kernel, plan), out_shape=(jax.Shap...  65.1 us
    pallas_call x1, Pallas kernels, block(): pl.pallas_call(functools.partial(block_kernel, plan), out_shape=(jax.Shap...  25.5 us
    pallas_call x1, Pallas kernels, enter_frame(): pl.pallas_call(functools.partial(enter_kernel, plan), out_shape=jax.Shape...  14.9 us
    unnamed x5, local copies, waits for them, and re-layouts  4.37 us
    pallas_call x2, local copies, waits for them, and re-layouts, write(): pl.pallas_call(functools.partial(write_kernel, plan, factor), out_shape=(...  3.88 us
    pallas_call x1, Pallas kernels, write(): pl.pallas_call(functools.partial(write_kernel, plan, factor), out_shape=(...  3.37 us

profile of v1, /device:TPU:1, one launch (start us, length us, event | category | flops | bytes accessed | tf_op | source)
XLA Modules:
  0.0 117.7 jit_solution(14859320789163423018)
XLA Ops:
  0.6 0.0 copy-start
  0.6 1.7 %copy.22.x_ref = bf16[8,6,2304]{2,1,0:T(8,128)(2,1)} copy(bf16[8,6,2304]{2,0,1:T(8,128)(2,1)} %param.16) | data formatting | bytes 442368 | tf_op args[0]
  2.4 1.7 %copy.23.g_ref = bf16[8,6,2304]{2,1,0:T(8,128)(2,1)} copy(bf16[8,6,2304]{2,0,1:T(8,128)(2,1)} %param.17) | data formatting | bytes 442368 | tf_op args[1]
  4.1 14.9 %enter_frame.1.frame_ref = bf16[4,160,384]{2,1,0:T(8,128)(2,1)} custom-call(bf16[8,6,2304]{2,1,0:T(8,128)(2,1)} %copy.22.x_ref, bf16[8,6,2304]{2,1,0:T(8,128)(2,1)} %copy.23.g_ref, s32[1,12]{1,0:T(1,128)} %bitcast.1, bf16[48,64]{1,0:T(8,128)(2,1)} %constant.14.clone.slab_ref), custom_call_target="tpu_custom_call" | custom-call | tf_op jit(solution)/shard_map/enter_frame/pallas_call | solution.py:199
  18.9 0.0 copy-done
  19.0 0.9 copy.24.w_down
  19.9 25.5 %block.1 = (bf16[4,144,192]{2,1,0:T(8,128)(2,1)}, bf16[2,16,7,16,128]{4,3,2,1,0:T(8,128)(2,1)}, bf16[2,2,14,16,128]{4,3,2,1,0:T(8,128)(2,1)}) custom-call(bf16[4,160,384]{2,1,0:T(8,128)(2,1)} %enter_frame.1.frame_ref, bf16[192,576]{1,0:T(8,128)(2,1)} %w_qkv.1, bf16[192,192]{1,0:T(8,128)(2,1)} %w_proj.1, bf16[192,768]{1,0:T(8,128)(2,1)} %w_up.1, ...), custom_call_target="tpu_custom_call" | custom-call | tf_op jit(solution)/shard_map/block/pallas_call | solution.py:399
  45.4 65.1 %share.1 = (bf16[4,144,192]{2,1,0:T(8,128)(2,1)}, bf16[2,16,7,16,128]{4,3,2,1,0:T(8,128)(2,1)}, bf16[2,2,14,16,128]{4,3,2,1,0:T(8,128)(2,1)}) custom-call(bf16[4,144,192]{2,1,0:T(8,128)(2,1)} %get-tuple-element.12.dx_ref, bf16[2,16,7,16,128]{4,3,2,1,0:T(8,128)(2,1)} %get-tuple-element.13.wsend, bf16[2,2,14,16,128]{4,3,2,1,0:T(8,128)(2,1)} %get-tuple-element.14.tsend), custom_call_target="tpu_custom_call" | custom-call | tf_op jit(solution)/shard_map/share/pallas_call | solution.py:641
  110.5 3.4 %write.1 = (bf16[8,6,2304]{2,1,0:T(8,128)(2,1)}, f32[192,576]{1,0:T(8,128)}, f32[192,192]{1,0:T(8,128)}, f32[192,768]{1,0:T(8,128)}, f32[768,192]{1,0:T(8,128)}, /*index=5*/f32[4,19872]{1,0:T(4,128)}) custom-call(bf16[4,144,192]{2,1,0:T(8,128)(2,1)} %get-tuple-element.15.home_ref, bf16[2,16,7,16,128]{4,3,2,1,0:T(8,128)(2,1)} %get-tuple-element.16.wall, ...), custom_call_target="tpu_custom_call" | custom-call | tf_op jit(solution)/shard_map/write/pallas_call | solution.py:718
  113.9 1.7 %copy.25 = bf16[8,6,2304]{2,0,1:T(8,128)(2,1)} copy(bf16[8,6,2304]{2,1,0:T(8,128)(2,1)} %get-tuple-element.18) | data formatting | bytes 442368 | tf_op jit(solution)/shard_map/write/pallas_call | solution.py:718
  115.5 2.2 %copy.26 = f32[768,192]{0,1:T(8,128)} copy(f32[768,192]{1,0:T(8,128)} %get-tuple-element.22) | data formatting | bytes 1179648 | tf_op jit(solution)/shard_map/write/pallas_call | solution.py:718
Async XLA Ops:
  0.6 18.3 %copy-start = (bf16[768,192]{0,1:T(8,128)(2,1)S(1)}, bf16[768,192]{0,1:T(8,128)(2,1)}, u32[]{:S(2)}) copy-start(bf16[768,192]{0,1:T(8,128)(2,1)} %param.21) | copy-start | bytes 884740

commit v2 on v0

v2 whole, which is shorter than its diff:
```python
import functools

import jax
import jax.numpy as jnp
import numpy as np
from jax import lax
from jax.experimental import pallas as pl
from jax.experimental.pallas import tpu as pltpu
from jax.sharding import PartitionSpec as P

F32 = jnp.float32
BF16 = jnp.bfloat16
MESH = pl.DeviceIdType.MESH

C = 192
HEADS = 6
HEAD_DIM = 32
MLP = 768
WZ = 2
WH = 6
WW = 12
LEVELS = 8
WIN = WZ * WH * WW
NWIN = LEVELS // WZ
CELLS = WIN * NWIN
CH = WW // 2
RH = WH // 2
SLAB = LEVELS * RH
QUARTER = CH * SLAB
PACK = 2 * C
EXTRA = 16
SPAN = 2 * WW - 1
ZR = WZ * WH
PAIRS = WW // 2
STRIP = 2 * ZR
TROWS = NWIN * HEADS * ZR
TCOLS = ZR * SPAN
TSEG = WH * SPAN
ECOLS = 1792
LCOLS = 640
KCOLS = (SPAN + 1) * ZR
TLANES = -(-TCOLS // 128)
TTILES = (TROWS // 16) * TLANES
XL = 2
NORM_EPS = 1e-5
MASKED = -1e30
VMEM_LIMIT = 56 * 1024 * 1024


def up_to(value, unit):
    return -(-value // unit) * unit


class Plan:
    def __init__(self, lon, lat):
        self.lon, self.lat = lon, lat
        self.nz = lon // (2 * XL)
        self.plane = XL * lat
        self.tt = -(-TTILES // (2 * XL))
        self.trows = self.tt * 16 // self.nz
        assert self.trows * self.nz == self.tt * 16

    def weight_tiles(self, columns):
        tiles = -(-(C // 16) * (columns // 128) // (2 * self.plane))
        while tiles * 16 % self.nz:
            tiles += 1
        return tiles


def cell_order():
    perm = np.zeros((CELLS, CELLS), np.float32)
    for w in range(NWIN):
        for c in range(WW):
            for z in range(WZ):
                for r in range(WH):
                    row = w * WIN + c * ZR + z * WH + r
                    quarter = (r // RH) * 2 + c // CH
                    col = quarter * QUARTER + (c % CH) * SLAB + w * WZ * RH + z * RH + r % RH
                    perm[row, col] = 1
    return perm


def slab_order():
    perm = np.zeros((2 * SLAB, LEVELS * WH), np.float32)
    for rs in range(2):
        for w in range(NWIN):
            for z in range(WZ):
                for r in range(RH):
                    row = rs * SLAB + w * WZ * RH + z * RH + r
                    perm[row, (rs * RH + r) * LEVELS + (2 * w + z + WZ // 2) % LEVELS] = 1
    return perm


def table_rows(odd):
    perm = np.zeros((2 * TROWS, TROWS), np.float32)
    for t in range(NWIN):
        for h in range(HEADS):
            for b in range(ZR):
                perm[((t * HEADS + h) * 2 + odd) * ZR + b, (h * ZR + b) * NWIN + t] = 1
    return perm


def table_lanes(odd):
    perm = np.zeros((TCOLS, KCOLS), np.float32)
    for b in range(ZR):
        for d in range(SPAN):
            perm[b * SPAN + d, (SPAN - 1 - d + odd) * ZR + b] = 1
    return perm


def table_sums():
    hit = np.zeros((PAIRS, WIN, KCOLS), np.float32)
    for pair in range(PAIRS):
        for cj in range(WW):
            for b in range(ZR):
                hit[pair, cj * ZR + b, (cj - 2 * pair + WW - 1) * ZR + b] = 1
    return hit


def column_of_cell():
    hit = np.zeros((WIN, EXTRA), np.float32)
    for c in range(WW):
        hit[c * ZR : (c + 1) * ZR, c] = 1
    return hit


def dot(a, b):
    return lax.dot_general(a, b, (((1,), (0,)), ((), ())), preferred_element_type=F32)


def dot_nt(a, b):
    return lax.dot_general(a, b, (((1,), (1,)), ((), ())), preferred_element_type=F32)


def dot_tn(a, b):
    return lax.dot_general(a, b, (((0,), (0,)), ((), ())), preferred_element_type=F32)


def neighbours(plan):
    lon, lat = lax.axis_index("lon"), lax.axis_index("lat")
    lon_b, lon_a = lax.rem(lon + plan.lon - 1, plan.lon), lax.rem(lon + 1, plan.lon)
    lat_b, lat_a = lax.rem(lat + plan.lat - 1, plan.lat), lax.rem(lat + 1, plan.lat)
    before = [(lon_b, lat), (lon, lat_b), (lon_b, lat_b)]
    after = [(lon_a, lat), (lon, lat_a), (lon_a, lat_a)]
    return before, after


def remote(src, dst, send, recv, place):
    return pltpu.make_async_remote_copy(
        src_ref=src, dst_ref=dst, send_sem=send, recv_sem=recv,
        device_id={"lon": place[0], "lat": place[1]}, device_id_type=MESH,
    )


def greet(place):
    pl.semaphore_signal(
        pltpu.get_barrier_semaphore(), inc=1,
        device_id={"lon": place[0], "lat": place[1]}, device_id_type=MESH,
    )


def each(first, last, act):
    def step(i, carry):
        act(i)
        return carry

    lax.fori_loop(first, last, step, 0)


class Spot:
    def __init__(self, plan):
        self.plan = plan
        self.lon, self.lat = lax.axis_index("lon"), lax.axis_index("lat")
        self.nz, self.plane = plan.nz, plan.plane
        self.core = lax.rem(self.lon, 2)
        self.z = lax.rem(self.lon // 2, self.nz)
        self.xl = self.lon // (2 * self.nz)
        self.me = self.xl * plan.lat + self.lat
        self.other = self.at(self.me, self.z, 1 - self.core)
        self.across = self.at((1 - self.xl) * plan.lat + self.lat, self.z, self.core)

    def at(self, p, z, core):
        return (p // self.plan.lat) * (2 * self.nz) + z * 2 + core, lax.rem(p, self.plan.lat)

    def plane_peer(self, d):
        return lax.rem(self.me + d, self.plane)

    def plane_from(self, d):
        return lax.rem(self.me - d + self.plane, self.plane)

    def z_peer(self, d):
        return lax.rem(self.z + d, self.nz)

    def greet_all(self):
        greet(self.other)
        each(1, self.plane, lambda d: greet(self.at(self.plane_peer(d), self.z, self.core)))
        each(1, self.nz, lambda d: greet(self.at(self.me, self.z_peer(d), self.core)))
        return 1 + self.plane - 1 + self.nz - 1


class Sum:
    def __init__(self, plan, columns, table):
        self.plan, self.table = plan, table
        self.columns = columns
        self.wt = plan.weight_tiles(columns)
        self.tt = plan.tt if table else 0
        self.wr = self.wt * 16 // plan.nz
        self.tr = plan.trows if table else 0
        self.zr = up_to(self.wr + self.tr, 16)

    def out_shapes(self):
        plan = self.plan
        shapes = [jax.ShapeDtypeStruct((2, plan.plane, self.wt, 16, 128), BF16)]
        if self.table:
            shapes.append(jax.ShapeDtypeStruct((2, XL, self.tt, 16, 128), BF16))
        return shapes

    def scratch(self):
        plan, wt, tt = self.plan, self.wt, self.tt
        plane, nz = plan.plane, plan.nz
        sem = pltpu.SemaphoreType.DMA
        shapes = dict(
            wsend=pltpu.VMEM((2, plane, wt, 16, 128), BF16),
            wr1=pltpu.VMEM((plane, wt, 16, 128), BF16),
            w1=pltpu.VMEM((plane, wt, 16, 128), BF16),
            wr2=pltpu.VMEM((plane, wt, 16, 128), BF16),
            wall=pltpu.VMEM((2, plane, wt, 16, 128), BF16),
            rows=pltpu.VMEM(((wt + tt) * 16, 128), F32),
            zrows=pltpu.VMEM((nz, self.zr, 128), F32),
            zsend=pltpu.VMEM((nz, self.zr, 128), BF16),
            zrecv=pltpu.VMEM((nz, self.zr, 128), BF16),
            zall=pltpu.VMEM((nz, self.zr, 128), BF16),
            c1s=sem((2,)), c1r=sem((2,)), p2s=sem((plane,)), p2r=sem((plane,)),
            z1s=sem((nz,)), z1r=sem((nz,)), z2s=sem((nz,)), z2r=sem((nz,)),
            p3s=sem((plane,)), p3r=sem((plane,)), c4s=sem((plane + 2,)), c4r=sem((plane + 2,)),
        )
        if self.table:
            shapes.update(
                tsend=pltpu.VMEM((2, XL, tt, 16, 128), BF16),
                tr1=pltpu.VMEM((XL, tt, 16, 128), BF16),
                t1=pltpu.VMEM((tt, 16, 128), BF16),
                tr2=pltpu.VMEM((tt, 16, 128), BF16),
                tall=pltpu.VMEM((2, XL, tt, 16, 128), BF16),
                t2s=sem((1,)), t2r=sem((1,)), t3s=sem((1,)), t3r=sem((1,)),
            )
        self.names = list(shapes)
        return list(shapes.values())

    def bind(self, spot, refs):
        self.spot = spot
        for name, ref in zip(self.names, refs):
            setattr(self, name, ref)

    def core_copies(self):
        s = self.spot
        copies = [remote(self.wsend.at[1 - s.core], self.wr1, self.c1s.at[0], self.c1r.at[0], s.other)]
        if self.table:
            copies.append(remote(self.tsend.at[1 - s.core], self.tr1, self.c1s.at[1], self.c1r.at[1], s.other))
        return copies

    def piece(self, d):
        s = self.spot
        p = s.plane_peer(d)
        return remote(self.w1.at[p], self.wr2.at[d], self.p2s.at[d], self.p2r.at[d], s.at(p, s.z, s.core))

    def table_piece(self):
        return remote(self.t1, self.tr2, self.t2s.at[0], self.t2r.at[0], self.spot.across)

    def z_out(self, d):
        s = self.spot
        p = s.z_peer(d)
        return remote(self.zsend.at[p], self.zrecv.at[d], self.z1s.at[d], self.z1r.at[d], s.at(s.me, p, s.core))

    def z_home(self, d):
        s = self.spot
        mine = self.zall.at[s.z]
        return remote(mine, mine, self.z2s.at[d], self.z2r.at[d], s.at(s.me, s.z_peer(d), s.core))

    def spread(self, d):
        s = self.spot
        mine = self.wall.at[s.core, s.me]
        return remote(mine, mine, self.p3s.at[d], self.p3r.at[d], s.at(s.plane_peer(d), s.z, s.core))

    def table_spread(self):
        s = self.spot
        mine = self.tall.at[s.core, s.xl]
        return remote(mine, mine, self.t3s.at[0], self.t3r.at[0], s.across)

    def hand(self, d):
        s = self.spot
        held = self.wall.at[s.core, s.plane_from(d)]
        return remote(held, held, self.c4s.at[d], self.c4r.at[d], s.other)

    def table_hand(self, i):
        s = self.spot
        held = self.tall.at[s.core, s.xl if i == 0 else 1 - s.xl]
        n = self.plan.plane + i
        return remote(held, held, self.c4s.at[n], self.c4r.at[n], s.other)

    def fill(self, total, table=None):
        plan = self.plan
        jobs = [(total, self.wsend, self.columns // 128, C // 16, plan.plane, self.wt)]
        if self.table:
            jobs.append((table, self.tsend, TLANES, TROWS // 16, XL, self.tt))
        for ref, out, lanes, rows, parts, tiles in jobs:
            for i in range(2 * parts * tiles):
                core, rest = divmod(i, parts * tiles)
                place = (core, rest // tiles, rest % tiles)
                if i < rows * lanes:
                    r, l = divmod(i, lanes)
                    out[place] = ref[r * 16 : r * 16 + 16, l * 128 : l * 128 + 128].astype(BF16)
                else:
                    out[place] = jnp.zeros((16, 128), BF16)

    def core_start(self):
        for copy in self.core_copies():
            copy.start()

    def plane_start(self):
        s = self.spot
        for copy in self.core_copies():
            copy.wait_recv()

        def send(d):
            p = s.plane_peer(d)
            self.w1[p] = (self.wsend[s.core, p].astype(F32) + self.wr1[p].astype(F32)).astype(BF16)
            self.piece(d).start()

        if self.table:
            far = 1 - s.xl
            self.t1[...] = (self.tsend[s.core, far].astype(F32) + self.tr1[far].astype(F32)).astype(BF16)
            self.table_piece().start()
        each(1, s.plane, send)

    def z_start(self):
        s, plan = self.spot, self.plan
        wlen = self.wt * 16

        def take(d, acc):
            self.piece(d).wait_recv()
            return acc + self.wr2[d].astype(F32)

        first = self.wsend[s.core, s.me].astype(F32) + self.wr1[s.me].astype(F32)
        self.rows[:wlen, :] = lax.fori_loop(1, s.plane, take, first).reshape(wlen, 128)
        if self.table:
            self.table_piece().wait_recv()
            near = self.tsend[s.core, s.xl].astype(F32) + self.tr1[s.xl].astype(F32)
            self.rows[wlen:, :] = (near + self.tr2[...].astype(F32)).reshape(self.tt * 16, 128)
        wr, tr = self.wr, self.tr
        if wr + tr < self.zr:
            self.zrows[...] = jnp.zeros_like(self.zrows)
        for i in range(s.nz):
            self.zrows[i, :wr, :] = self.rows[i * wr : (i + 1) * wr, :]
            if tr:
                self.zrows[i, wr : wr + tr, :] = self.rows[wlen + i * tr : wlen + (i + 1) * tr, :]
        self.zsend[...] = self.zrows[...].astype(BF16)
        each(1, s.nz, lambda d: self.z_out(d).start())

    def z_back(self):
        s = self.spot

        def take(d, acc):
            self.z_out(d).wait_recv()
            return acc + self.zrecv[d].astype(F32)

        self.zall[s.z] = lax.fori_loop(1, s.nz, take, self.zsend[s.z].astype(F32)).astype(BF16)
        each(1, s.nz, lambda d: self.z_home(d).start())

    def plane_back(self):
        s, plan = self.spot, self.plan
        each(1, s.nz, lambda d: self.z_home(d).wait_recv())
        self.zrows[...] = self.zall[...].astype(F32)
        wr, tr, wlen = self.wr, self.tr, self.wt * 16
        for i in range(s.nz):
            self.rows[i * wr : (i + 1) * wr, :] = self.zrows[i, :wr, :]
            if tr:
                self.rows[wlen + i * tr : wlen + (i + 1) * tr, :] = self.zrows[i, wr : wr + tr, :]
        if self.table:
            self.tall[s.core, s.xl] = self.rows[wlen:, :].astype(BF16).reshape(self.tt, 16, 128)
            self.table_spread().start()
            self.table_hand(0).start()
        self.wall[s.core, s.me] = self.rows[:wlen, :].astype(BF16).reshape(self.wt, 16, 128)
        each(1, s.plane, lambda d: self.spread(d).start())
        self.hand(0).start()

    def hand_over(self):
        if self.table:
            self.table_spread().wait_recv()
            self.table_hand(1).start()

        def forward(d):
            self.spread(d).wait_recv()
            self.hand(d).start()

        each(1, self.spot.plane, forward)

    def finish(self):
        each(0, self.spot.plane, lambda d: self.hand(d).wait_recv())
        if self.table:
            self.table_hand(0).wait_recv()
            self.table_hand(1).wait_recv()

    def drain(self):
        s = self.spot
        for copy in self.core_copies():
            copy.wait_send()
        if self.table:
            for copy in (self.table_piece(), self.table_spread(), self.table_hand(0), self.table_hand(1)):
                copy.wait_send()

        def plane(d):
            self.piece(d).wait_send()
            self.spread(d).wait_send()

        def over_z(d):
            self.z_out(d).wait_send()
            self.z_home(d).wait_send()

        each(1, s.plane, plane)
        each(1, s.nz, over_z)
        each(0, s.plane, lambda d: self.hand(d).wait_send())


def normed_of(v):
    centred = v - jnp.mean(v, axis=-1, keepdims=True)
    inv = lax.rsqrt(jnp.mean(centred * centred, axis=-1, keepdims=True) + NORM_EPS)
    return centred * inv, inv


def norm_back(up, normed, inv):
    return inv * (
        up
        - jnp.mean(up, axis=-1, keepdims=True)
        - normed * jnp.mean(up * normed, axis=-1, keepdims=True)
    )


FAR = (
    "w_qkv", "w_proj", "w_up", "w_downt", "order", "back",
    "even_row", "odd_row", "even_lane", "odd_lane", "tsum", "ccol",
)
QUARTERS = (4, QUARTER + EXTRA, PACK)
SCRATCH = dict(
    packed=(QUARTERS, F32),
    outward=(QUARTERS, BF16),
    frame=(QUARTERS, BF16),
    tn=((TROWS, TCOLS), F32),
    spread=((2 * TROWS, KCOLS), F32),
    bars=((2, WIN, WIN), F32),
    xs=((CELLS, C), F32),
    gm=((CELLS, C), BF16),
    act=((CELLS, C), BF16),
    q=((CELLS, C), BF16),
    k=((CELLS, C), BF16),
    v=((CELLS, C), BF16),
    qkvt=((NWIN, 3 * C, WIN), BF16),
    ot=((NWIN, C, WIN), BF16),
    dot=((NWIN, C, WIN), BF16),
    dh=((CELLS, C), BF16),
    dout=((CELLS, C), BF16),
    b=((CELLS, C), BF16),
    m=((CELLS, MLP), BF16),
    du=((CELLS, MLP), BF16),
    dqkvt=((3 * C, WIN), BF16),
    back=((CELLS, C), F32),
    wqkvt=((3 * C, C), BF16),
    bias=((NWIN * HEADS, WIN, WIN), F32),
    prob=((NWIN * HEADS, WIN, WIN), F32),
    dcol=((PAIRS, 2 * TROWS, WIN), BF16),
    early=((C, ECOLS), F32),
    late=((C, LCOLS), F32),
    lsum=((3 * C, C), F32),
    tgrad=((TROWS, TLANES * 128), F32),
    send=((4, QUARTER, C), BF16),
    hrecv=((4, QUARTER, C), BF16),
)


def block_kernel(plan, sums, *refs):
    x_ref, g_ref, valid_ref, slab_ref, table_ref = refs[:5]
    far = refs[5 : 5 + len(FAR)]
    refs = refs[5 + len(FAR) :]
    home_ref, early_ref, late_ref, tall_ref = refs[:4]
    near = dict(zip(FAR, refs[4 : 4 + len(FAR)]))
    refs = refs[4 + len(FAR) :]
    s = dict(zip(SCRATCH, refs))
    refs = refs[len(SCRATCH) :]
    fs, es, er, hs, hr, outs = refs[:6]
    refs = refs[6:]
    spot = Spot(plan)
    early, late = sums
    early.bind(spot, refs[: len(early.names)])
    late.bind(spot, refs[len(early.names) :])
    before, after = neighbours(plan)
    for place in before + after:
        greet(place)
    greeted = spot.greet_all() + 6
    fetch = [pltpu.make_async_copy(src, near[name], fs.at[n]) for n, (name, src) in enumerate(zip(FAR, far))]
    for copy in fetch:
        copy.start()
    w_qkv, w_proj, w_up, w_downt, order_ref, back_ref, tsum_ref, ccol_ref = (
        near[n] for n in ("w_qkv", "w_proj", "w_up", "w_downt", "order", "back", "tsum", "ccol")
    )

    hm = []
    lane = lax.broadcasted_iota(jnp.int32, (1, C), 1)
    for h in range(HEADS):
        hm.append(jnp.where(lane // HEAD_DIM == h, 1.0, 0.0).astype(BF16))
    scale = HEAD_DIM ** (-0.5)

    slab = slab_ref[...]
    packed, outward, frame = s["packed"], s["outward"], s["frame"]
    packed[:, QUARTER:, :] = jnp.zeros((4, EXTRA, PACK), F32)
    for part, ref in enumerate((x_ref, g_ref)):
        rows = dot(slab, ref[...])
        for c in range(WW):
            for rs in range(2):
                piece = rows[rs * SLAB : (rs + 1) * SLAB, c * C : (c + 1) * C]
                if part == 1:
                    piece = piece * valid_ref[0, c].astype(F32)
                packed[
                    rs * 2 + c // CH, (c % CH) * SLAB : (c % CH + 1) * SLAB, part * C : (part + 1) * C
                ] = piece
    for c in range(WW):
        mark = jnp.full((1, PACK), valid_ref[0, c].astype(F32), F32)
        for rs in range(2):
            packed[rs * 2 + c // CH, QUARTER + c % CH : QUARTER + c % CH + 1, :] = mark
    outward[...] = packed[...].astype(BF16)
    for h in range(HEADS):
        for zi in range(WZ):
            for zj in range(WZ):
                for ri in range(WH):
                    seg = ((h * WZ + zi) * WZ + zj) * WH + ri
                    row = (h * ZR + zi * WH + ri) * NWIN
                    s["tn"][row : row + NWIN, zj * TSEG : (zj + 1) * TSEG] = table_ref[
                        :, seg * TSEG : (seg + 1) * TSEG
                    ]
    pl.semaphore_wait(pltpu.get_barrier_semaphore(), greeted)
    enter = [
        remote(outward.at[2], frame.at[1], es.at[0], er.at[0], before[0]),
        remote(outward.at[1], frame.at[2], es.at[1], er.at[1], before[1]),
        remote(outward.at[0], frame.at[3], es.at[2], er.at[2], before[2]),
    ]
    for copy in enter:
        copy.start()
    frame[0] = outward[3]

    for copy in fetch:
        copy.wait()
    left = s["tn"][...]
    for n in range(3):
        term = left.astype(BF16)
        left = left - term.astype(F32)
        part = dot(dot_tn(near["even_row"][...], term).astype(BF16), near["even_lane"][...]) + dot(
            dot_tn(near["odd_row"][...], term).astype(BF16), near["odd_lane"][...]
        )
        if n == 0:
            s["spread"][...] = part
        else:
            s["spread"][...] += part
    for t in range(NWIN):
        for pair in range(PAIRS):
            first = (WW - 1 - 2 * pair) * ZR
            rows = s["spread"][t * HEADS * STRIP : (t + 1) * HEADS * STRIP, first : first + WIN]
            s["bias"][t * HEADS : (t + 1) * HEADS, pair * STRIP : (pair + 1) * STRIP, :] = rows.reshape(
                HEADS, STRIP, WIN
            )
    s["wqkvt"][...] = w_qkv[...].T
    ccol = ccol_ref[...]
    ii = lax.broadcasted_iota(jnp.int32, (WIN, WIN), 0)
    jj = lax.broadcasted_iota(jnp.int32, (WIN, WIN), 1)
    low_i, low_j = (lax.rem(ii, WH) >= RH).astype(jnp.int32), (lax.rem(jj, WH) >= RH).astype(jnp.int32)
    open_rows = jnp.where(lax.axis_index("lat") == plan.lat - 1, 0, 1)
    top_i, top_j = lax.rem(ii // WH, WZ), lax.rem(jj // WH, WZ)
    s["bars"][0] = jnp.where((low_i == low_j) | (open_rows == 1), 0.0, MASKED)
    s["bars"][1] = jnp.where(top_i == top_j, 0.0, MASKED)
    for copy in enter:
        copy.wait_recv()

    cells = dot(order_ref[...], frame[:, :QUARTER, :].reshape(CELLS, PACK))
    s["xs"][...] = cells[:, :C]
    s["gm"][...] = cells[:, C:].astype(BF16)

    marks = jnp.concatenate(
        [
            frame[0, QUARTER : QUARTER + EXTRA, :WIN][:CH].astype(F32),
            frame[1, QUARTER : QUARTER + EXTRA, :WIN][:CH].astype(F32),
            jnp.zeros((EXTRA - WW, WIN), F32),
        ],
        axis=0,
    ).astype(BF16)
    same = dot(ccol, marks) == lax.dot_general(
        marks, ccol, (((0,), (1,)), ((), ())), preferred_element_type=F32
    )
    barred = jnp.where(same, s["bars"][0], MASKED)
    s["bars"][0] = barred
    s["bars"][1] = jnp.minimum(barred, s["bars"][1])

    normed, inv = normed_of(s["xs"][...])
    a = normed.astype(BF16)
    s["act"][...] = a
    s["q"][...] = dot(a, w_qkv[:, :C]).astype(BF16)
    s["k"][...] = dot(a, w_qkv[:, C : 2 * C]).astype(BF16)
    s["v"][...] = dot(a, w_qkv[:, 2 * C :]).astype(BF16)

    def forward(w, carry):
        at = pl.ds(pl.multiple_of(w * WIN, WIN), WIN)
        q, k = s["q"][at, :], s["k"][at, :]
        bar = s["bars"][(w == NWIN - 1).astype(jnp.int32)]
        qkvt = dot_nt(s["wqkvt"][...], s["act"][at, :]).astype(BF16)
        s["qkvt"][w] = qkvt
        for h in range(HEADS):
            score = dot_nt(q * hm[h], k) * scale + s["bias"][w * HEADS + h] + bar
            e = jnp.exp(score - jnp.max(score, axis=-1, keepdims=True))
            p = e * (1.0 / jnp.sum(e, axis=-1, keepdims=True))
            s["prob"][w * HEADS + h] = p
            head = 2 * C + h * HEAD_DIM
            s["ot"][w, h * HEAD_DIM : (h + 1) * HEAD_DIM, :] = dot_nt(
                qkvt[head : head + HEAD_DIM, :], p.astype(BF16)
            ).astype(BF16)
        return carry

    lax.fori_loop(0, NWIN, forward, 0)

    def middle(w, carry):
        at = pl.ds(pl.multiple_of(w * WIN, WIN), WIN)
        mid = (s["xs"][at, :] + dot_tn(s["ot"][w], w_proj[...])).astype(BF16).astype(F32)
        n2, inv2 = normed_of(mid)
        b = n2.astype(BF16)
        s["b"][at, :] = b
        u = dot(b, w_up[...])
        cdf = 0.5 * (1.0 + lax.erf(u * 0.7071067811865476))
        s["m"][at, :] = (u * cdf).astype(BF16)
        slope = cdf + u * jnp.exp(-0.5 * u * u) * 0.3989422804014327
        g = s["gm"][at, :]
        du = (dot(g, w_downt[...]) * slope).astype(BF16)
        s["du"][at, :] = du
        dh = (g.astype(F32) + norm_back(dot_nt(du, w_up[...]), n2, inv2)).astype(BF16)
        s["dh"][at, :] = dh
        s["dout"][at, :] = dot_nt(dh, w_proj[...]).astype(BF16)
        s["dot"][w] = dot_nt(w_proj[...], dh).astype(BF16)
        return carry

    lax.fori_loop(0, NWIN, middle, 0)
    s["early"][:, :MLP] = dot_tn(s["b"][...], s["du"][...])
    s["early"][:, MLP : 2 * MLP] = dot_tn(s["gm"][...], s["m"][...])
    proj = jnp.zeros((C, C), F32)
    for w in range(NWIN):
        proj += dot(s["ot"][w], s["dh"][w * WIN : (w + 1) * WIN, :])
    s["early"][:, 2 * MLP : 2 * MLP + C] = proj
    s["early"][:, 2 * MLP + C :] = jnp.zeros((C, ECOLS - 2 * MLP - C), F32)
    early.fill(s["early"])
    early.core_start()

    for w in range(NWIN):
        at = pl.ds(w * WIN, WIN)
        k, v, do = s["k"][at, :], s["v"][at, :], s["dout"][at, :]
        for h in range(HEADS):
            p = s["prob"][w * HEADS + h]
            dp = dot_nt(do * hm[h], v)
            ds = p * (dp - jnp.sum(p * dp, axis=-1, keepdims=True))
            dsb = ds.astype(BF16)
            first = (w * HEADS + h) * STRIP
            for pair in range(PAIRS):
                s["dcol"][pair, first : first + STRIP, :] = dsb[pair * STRIP : (pair + 1) * STRIP, :]
            low, high = h * HEAD_DIM, (h + 1) * HEAD_DIM
            kt, qt = s["qkvt"][w, C + low : C + high, :], s["qkvt"][w, low:high, :]
            s["dqkvt"][low:high, :] = (dot_nt(kt, dsb) * scale).astype(BF16)
            s["dqkvt"][C + low : C + high, :] = (dot(qt, dsb) * scale).astype(BF16)
            s["dqkvt"][2 * C + low : 2 * C + high, :] = dot(s["dot"][w, low:high, :], p.astype(BF16)).astype(BF16)
        dqkvt = s["dqkvt"][...]
        s["back"][at, :] = dot(w_qkv[...], dqkvt).T
        term = dot(dqkvt, s["act"][at, :])
        if w == 0:
            s["lsum"][...] = term
        else:
            s["lsum"][...] += term
        if w == 0:
            early.plane_start()

    grad = jnp.zeros((2 * TROWS, KCOLS), F32)
    for pair in range(PAIRS):
        grad += dot(s["dcol"][pair], tsum_ref[pair])
    grad = grad.astype(BF16)
    s["tgrad"][...] = jnp.zeros_like(s["tgrad"])
    s["tgrad"][:, :TCOLS] = dot_nt(dot(near["even_row"][...], grad).astype(BF16), near["even_lane"][...]) + dot_nt(
        dot(near["odd_row"][...], grad).astype(BF16), near["odd_lane"][...]
    )
    s["late"][:, : 3 * C] = s["lsum"][...].T
    s["late"][:, 3 * C :] = jnp.zeros((C, LCOLS - 3 * C), F32)
    late.fill(s["late"], s["tgrad"])
    late.core_start()

    normed, inv = normed_of(s["xs"][...])
    dxs = (s["dh"][...].astype(F32) + norm_back(s["back"][...], normed, inv)).astype(BF16)
    s["send"][...] = dot(back_ref[...], dxs).astype(BF16).reshape(4, QUARTER, C)
    home = [
        remote(s["send"].at[1], s["hrecv"].at[2], hs.at[0], hr.at[0], after[0]),
        remote(s["send"].at[2], s["hrecv"].at[1], hs.at[1], hr.at[1], after[1]),
        remote(s["send"].at[3], s["hrecv"].at[0], hs.at[2], hr.at[2], after[2]),
    ]
    late.plane_start()
    for copy in home:
        copy.start()
    home_ref[3] = s["send"][0]

    early.z_start()
    late.z_start()
    early.z_back()
    late.z_back()
    early.plane_back()
    late.plane_back()
    early.hand_over()
    for copy in home:
        copy.wait_recv()
    for q in range(3):
        home_ref[q] = s["hrecv"][q]
    late.hand_over()
    early.finish()
    write_out = [pltpu.make_async_copy(early.wall, early_ref, outs.at[0])]
    write_out[0].start()
    late.finish()
    write_out.append(pltpu.make_async_copy(late.wall, late_ref, outs.at[1]))
    write_out.append(pltpu.make_async_copy(late.tall, tall_ref, outs.at[2]))
    write_out[1].start()
    write_out[2].start()
    for copy in enter + home:
        copy.wait_send()
    early.drain()
    late.drain()
    for copy in write_out:
        copy.wait()


def block(plan, state, cotangent, valid, table, w_qkv, w_proj, w_up, w_down):
    vmem = pl.BlockSpec(memory_space=pltpu.VMEM)
    hbm = pl.BlockSpec(memory_space=pl.ANY)
    order = cell_order()
    sums = (Sum(plan, ECOLS, False), Sum(plan, LCOLS, True))
    consts = (
        order, order.T, table_rows(0).T, table_rows(1).T, table_lanes(0), table_lanes(1),
        table_sums(), column_of_cell(),
    )
    far = [w_qkv, w_proj, w_up, w_down.T] + [jnp.asarray(m, BF16) for m in consts]
    scratch = [pltpu.VMEM(v.shape, v.dtype) for v in far]
    scratch += [pltpu.VMEM(shape, dtype) for shape, dtype in SCRATCH.values()]
    sem = pltpu.SemaphoreType.DMA
    scratch += [sem((len(FAR),)), sem((3,)), sem((3,)), sem((3,)), sem((3,)), sem((3,))]
    for one in sums:
        scratch += one.scratch()
    rows = lambda v: v.transpose(1, 0, 2).reshape(WH * LEVELS, WW * C)
    return pl.pallas_call(
        functools.partial(block_kernel, plan, sums),
        out_shape=[jax.ShapeDtypeStruct((4, QUARTER, C), BF16)] + sums[0].out_shapes() + sums[1].out_shapes(),
        in_specs=[vmem, vmem, pl.BlockSpec(memory_space=pltpu.SMEM), vmem, vmem] + [hbm] * len(far),
        out_specs=[vmem, hbm, hbm, hbm],
        scratch_shapes=scratch,
        compiler_params=pltpu.CompilerParams(
            collective_id=0, has_side_effects=True, vmem_limit_bytes=VMEM_LIMIT
        ),
        name="block",
    )(
        rows(state), rows(cotangent), valid.reshape(1, WW), jnp.asarray(slab_order(), BF16), table, *far
    )


def write_kernel(
    plan, factor, home_ref, early_ref, late_ref, tall_ref, slab_ref,
    dx_ref, qkv_ref, proj_ref, up_ref, down_ref, table_ref, band, early, late, tgrad,
):
    jobs = (
        (early_ref, early, ECOLS // 128, C // 16, plan.plane, factor),
        (late_ref, late, LCOLS // 128, C // 16, plan.plane, factor),
        (tall_ref, tgrad, TLANES, TROWS // 16, XL, 1.0),
    )
    for src, dst, lanes, rows, parts, gain in jobs:
        tiles = src.shape[2]
        for i in range(rows * lanes):
            core, rest = divmod(i, parts * tiles)
            r, l = divmod(i, lanes)
            value = src[core, rest // tiles, rest % tiles].astype(F32)
            dst[r * 16 : r * 16 + 16, l * 128 : l * 128 + 128] = value * gain if gain != 1.0 else value
    up_ref[...] = early[:, :MLP]
    down_ref[...] = early[:, MLP : 2 * MLP]
    proj_ref[...] = early[:, 2 * MLP : 2 * MLP + C]
    qkv_ref[...] = late[:, : 3 * C]
    for h in range(HEADS):
        for zi in range(WZ):
            for zj in range(WZ):
                for ri in range(WH):
                    seg = ((h * WZ + zi) * WZ + zj) * WH + ri
                    row = (h * ZR + zi * WH + ri) * NWIN
                    table_ref[:, seg * TSEG : (seg + 1) * TSEG] = tgrad[
                        row : row + NWIN, zj * TSEG : (zj + 1) * TSEG
                    ]
    for c in range(WW):
        for rs in range(2):
            band[rs * SLAB : (rs + 1) * SLAB, c * C : (c + 1) * C] = home_ref[
                rs * 2 + c // CH, (c % CH) * SLAB : (c % CH + 1) * SLAB, :
            ].astype(F32)
    dx_ref[...] = dot(slab_ref[...], band[...].astype(BF16)).astype(BF16)


def write(plan, home, early, late, tall):
    vmem = pl.BlockSpec(memory_space=pltpu.VMEM)
    factor = float(CELLS * plan.lon * plan.lat) ** (-0.5)
    dx, qkv, proj, up, down, table = pl.pallas_call(
        functools.partial(write_kernel, plan, factor),
        out_shape=(
            jax.ShapeDtypeStruct((WH * LEVELS, WW * C), BF16),
            jax.ShapeDtypeStruct((C, 3 * C), F32),
            jax.ShapeDtypeStruct((C, C), F32),
            jax.ShapeDtypeStruct((C, MLP), F32),
            jax.ShapeDtypeStruct((C, MLP), F32),
            jax.ShapeDtypeStruct((NWIN, HEADS * ZR * ZR * SPAN), F32),
        ),
        in_specs=[vmem] * 5,
        out_specs=(vmem,) * 6,
        scratch_shapes=[
            pltpu.VMEM((2 * SLAB, WW * C), F32),
            pltpu.VMEM((C, ECOLS), F32),
            pltpu.VMEM((C, LCOLS), F32),
            pltpu.VMEM((TROWS, TLANES * 128), F32),
        ],
        compiler_params=pltpu.CompilerParams(vmem_limit_bytes=VMEM_LIMIT),
        name="write",
    )(home, early, late, tall, jnp.asarray(slab_order().T, BF16))
    dx = dx.reshape(WH, LEVELS, WW * C).transpose(1, 0, 2)
    return dx, qkv, proj, up, down.T, table


def per_device(plan, state_in, cotangent, w_qkv, w_proj, w_up, w_down, bias_table, pad_valid):
    return write(plan, *block(plan, state_in, cotangent, pad_valid, bias_table, w_qkv, w_proj, w_up, w_down))


def solution(mesh):
    plan = Plan(mesh.shape["lon"], mesh.shape["lat"])
    return jax.shard_map(
        functools.partial(per_device, plan),
        mesh=mesh,
        in_specs=(
            P(None, "lat", "lon"),
            P(None, "lat", "lon"),
            P(),
            P(),
            P(),
            P(),
            P("lat", None),
            P("lon"),
        ),
        out_specs=(P(None, "lat", "lon"), P(), P(), P(), P(), P("lat", None)),
        check_vma=False,
    )
```

time: 1060 us -> 90.4 us (0.09)
  waiting for transfers between devices: 863 us -> 0 us
  Pallas kernels: 0 us -> 89.6 us
  local copies, waits for them, and re-layouts: 61.6 us -> 0 us
  matrix products: 45.3 us -> 0 us
  starting transfers between devices: 43.6 us -> 0 us
  other arithmetic: 24.1 us -> 0 us
  between operations: 15.2 us -> 0.64 us
    psum x2 -> x0, waiting for transfers between devices: 843 us -> none  [the longest x1 449 us: per_device(): lax.psum((qkv_part, proj_part, up_part, down_part), ('lon', 'lat'))]
    pallas_call x0 -> x2, Pallas kernels: none -> 89.6 us  [the longest x1 86.5 us: block(): pl.pallas_call(functools.partial(block_kernel, plan, sums), out_shape=[ja...]
    dot_general x20 -> x0, matrix products: 45.3 us -> none  [the longest x6 16.9 us: batched(): jnp.einsum(formula, left_op, right_op, preferred_element_type=jnp.float32)]
    ppermute x10 -> x0, starting transfers between devices: 43.3 us -> none  [passed_along(): return lax.ppermute(value, axis, pairs)]
    ppermute x10 -> x0, waiting for transfers between devices: 19.7 us -> none  [passed_along(): return lax.ppermute(value, axis, pairs)]
    convert_element_type x8 -> x0, local copies, waits for them, and re-layouts: 15.8 us -> none  [the longest x4 13.2 us: attend_back(): jnp.stack([query_grad, key_grad, value_grad], axis=2).astype(jnp.bfloat16)]
    reshape x7 -> x0, local copies, waits for them, and re-layouts: 13.2 us -> none  [the longest x2 8.47 us: window_bias(): return spread.reshape(window_count, HEADS, window_cells, window_cells)]
    and x7 -> x0, local copies, waits for them, and re-layouts: 11.4 us -> none  [spread_table(): (row_level == col_level) & (row_lat == col_lat)]
  transfers between devices with their start and end apart: 12 -> 0, of which waited for: 6 -> 0; matrix products, arithmetic and copies ran while one was open for 7% -> 0% of each run, Pallas kernels for 0% -> 0%
where the time goes in v2:
time: 90.4 us; the launch traced here: 90.2 us
  Pallas kernels  89.6 us (99%)
    pallas_call x1, Pallas kernels, block(): pl.pallas_call(functools.partial(block_kernel, plan, sums), out_shape=[ja...  86.5 us
    pallas_call x1, Pallas kernels, write(): pl.pallas_call(functools.partial(write_kernel, plan, factor), out_shape=(...  3.05 us

profile of v2, /device:TPU:1, one launch (start us, length us, event | category | flops | bytes accessed | tf_op | source)
XLA Modules:
  0.0 90.2 jit_solution(16727813523269442939)
XLA Ops:
  0.6 86.5 %block.1 = (bf16[4,144,192]{2,1,0:T(8,128)(2,1)}, bf16[2,16,6,16,128]{4,3,2,1,0:T(8,128)(2,1)}, bf16[2,16,2,16,128]{4,3,2,1,0:T(8,128)(2,1)}, bf16[2,2,14,16,128]{4,3,2,1,0:T(8,128)(2,1)}) custom-call(bf16[48,2304]{1,0:T(8,128)(2,1)} %bitcast.13, bf16[48,2304]{1,0:T(8,128)(2,1)} %bitcast.14, s32[1,12]{1,0:T(1,128)} %bitcast.15, ...), custom_call_target="tpu_custom_call" | custom-call | tf_op jit(solution)/shard_map/block/pallas_call | solution.py:752
  87.1 3.1 %write.1 = (bf16[48,2304]{1,0:T(8,128)(2,1)}, f32[192,576]{1,0:T(8,128)}, f32[192,192]{1,0:T(8,128)}, f32[192,768]{1,0:T(8,128)}, f32[192,768]{1,0:T(8,128)}, /*index=5*/f32[4,19872]{1,0:T(4,128)}) custom-call(bf16[4,144,192]{2,1,0:T(8,128)(2,1)} %get-tuple-element.16.home_ref, bf16[2,16,6,16,128]{4,3,2,1,0:T(8,128)(2,1)} %get-tuple-element.17.early_ref, ...), custom_call_target="tpu_custom_call" | custom-call | tf_op jit(solution)/shard_map/write/pallas_call | solution.py:807

commit v3 on v2

v3 whole, which is shorter than its diff:
```python
import functools

import jax
import jax.numpy as jnp
import numpy as np
from jax import lax
from jax.experimental import pallas as pl
from jax.experimental.pallas import tpu as pltpu
from jax.sharding import PartitionSpec as P

F32 = jnp.float32
BF16 = jnp.bfloat16
MESH = pl.DeviceIdType.MESH

C = 192
HEADS = 6
HEAD_DIM = 32
MLP = 768
WZ = 2
WH = 6
WW = 12
LEVELS = 8
WIN = WZ * WH * WW
NWIN = LEVELS // WZ
CELLS = WIN * NWIN
CH = WW // 2
RH = WH // 2
SLAB = LEVELS * RH
QUARTER = CH * SLAB
PACK = 2 * C
EXTRA = 16
SPAN = 2 * WW - 1
ZR = WZ * WH
PAIRS = WW // 2
STRIP = 2 * ZR
TROWS = NWIN * HEADS * ZR
TCOLS = ZR * SPAN
TSEG = WH * SPAN
DOWN = 512
ECOLS = MLP + DOWN
LCOLS = 4 * C + MLP - DOWN
KCOLS = (SPAN + 1) * ZR
TLANES = -(-TCOLS // 128)
TTILES = (TROWS // 16) * TLANES
XL = 2
NORM_EPS = 1e-5
MASKED = -1e30
VMEM_LIMIT = 56 * 1024 * 1024


def up_to(value, unit):
    return -(-value // unit) * unit


class Plan:
    def __init__(self, lon, lat):
        self.lon, self.lat = lon, lat
        self.nz = lon // (2 * XL)
        self.plane = XL * lat
        self.tt = -(-TTILES // (2 * XL))
        self.trows = self.tt * 16 // self.nz
        assert self.trows * self.nz == self.tt * 16

    def weight_tiles(self, columns):
        tiles = -(-(C // 16) * (columns // 128) // (2 * self.plane))
        while tiles * 16 % self.nz:
            tiles += 1
        return tiles


def cell_order():
    perm = np.zeros((CELLS, CELLS), np.float32)
    for w in range(NWIN):
        for c in range(WW):
            for z in range(WZ):
                for r in range(WH):
                    row = w * WIN + c * ZR + z * WH + r
                    quarter = (r // RH) * 2 + c // CH
                    col = quarter * QUARTER + (c % CH) * SLAB + w * WZ * RH + z * RH + r % RH
                    perm[row, col] = 1
    return perm


def slab_order():
    perm = np.zeros((2 * SLAB, LEVELS * WH), np.float32)
    for rs in range(2):
        for w in range(NWIN):
            for z in range(WZ):
                for r in range(RH):
                    row = rs * SLAB + w * WZ * RH + z * RH + r
                    perm[row, (rs * RH + r) * LEVELS + (2 * w + z + WZ // 2) % LEVELS] = 1
    return perm


def table_lanes(odd):
    perm = np.zeros((TCOLS, KCOLS), np.float32)
    for b in range(ZR):
        for d in range(SPAN):
            perm[b * SPAN + d, (SPAN - 1 - d + odd) * ZR + b] = 1
    return perm


def table_sums():
    hit = np.zeros((PAIRS, WIN, KCOLS), np.float32)
    for pair in range(PAIRS):
        for cj in range(WW):
            for b in range(ZR):
                hit[pair, cj * ZR + b, (cj - 2 * pair + WW - 1) * ZR + b] = 1
    return hit


def column_of_cell():
    hit = np.zeros((WIN, EXTRA), np.float32)
    for c in range(WW):
        hit[c * ZR : (c + 1) * ZR, c] = 1
    return hit


def segments(h, zi, ri):
    return [(((h * WZ + zi) * WZ + zj) * WH + ri) * TSEG for zj in range(WZ)]


def dot(a, b):
    return lax.dot_general(a, b, (((1,), (0,)), ((), ())), preferred_element_type=F32)


def dot_nt(a, b):
    return lax.dot_general(a, b, (((1,), (1,)), ((), ())), preferred_element_type=F32)


def dot_tn(a, b):
    return lax.dot_general(a, b, (((0,), (0,)), ((), ())), preferred_element_type=F32)


def neighbours(plan):
    lon, lat = lax.axis_index("lon"), lax.axis_index("lat")
    lon_b, lon_a = lax.rem(lon + plan.lon - 1, plan.lon), lax.rem(lon + 1, plan.lon)
    lat_b, lat_a = lax.rem(lat + plan.lat - 1, plan.lat), lax.rem(lat + 1, plan.lat)
    before = [(lon_b, lat), (lon, lat_b), (lon_b, lat_b)]
    after = [(lon_a, lat), (lon, lat_a), (lon_a, lat_a)]
    return before, after


def remote(src, dst, send, recv, place):
    return pltpu.make_async_remote_copy(
        src_ref=src, dst_ref=dst, send_sem=send, recv_sem=recv,
        device_id={"lon": place[0], "lat": place[1]}, device_id_type=MESH,
    )


def greet(place):
    pl.semaphore_signal(
        pltpu.get_barrier_semaphore(), inc=1,
        device_id={"lon": place[0], "lat": place[1]}, device_id_type=MESH,
    )


def each(first, last, act):
    def step(i, carry):
        act(i)
        return carry

    lax.fori_loop(first, last, step, 0)


class Spot:
    def __init__(self, plan):
        self.plan = plan
        self.lon, self.lat = lax.axis_index("lon"), lax.axis_index("lat")
        self.nz, self.plane = plan.nz, plan.plane
        self.core = lax.rem(self.lon, 2)
        self.z = lax.rem(self.lon // 2, self.nz)
        self.xl = self.lon // (2 * self.nz)
        self.me = self.xl * plan.lat + self.lat
        self.other = self.at(self.me, self.z, 1 - self.core)
        self.across = self.at((1 - self.xl) * plan.lat + self.lat, self.z, self.core)

    def at(self, p, z, core):
        return (p // self.plan.lat) * (2 * self.nz) + z * 2 + core, lax.rem(p, self.plan.lat)

    def at_plane(self, p):
        return self.at(p, self.z, self.core)

    def at_z(self, z):
        return self.at(self.me, z, self.core)

    def plane_peer(self, d):
        return lax.rem(self.me + d, self.plane)

    def z_peer(self, d):
        return lax.rem(self.z + d, self.nz)

    def greet_all(self):
        greet(self.other)
        each(1, self.plane, lambda d: greet(self.at_plane(self.plane_peer(d))))
        each(1, self.nz, lambda d: greet(self.at_z(self.z_peer(d))))
        return 1 + self.plane - 1 + self.nz - 1


def cut(src, out, lanes, rows, parts, tiles):
    for i in range(2 * parts * tiles):
        core, rest = divmod(i, parts * tiles)
        place = (core, rest // tiles, rest % tiles)
        if i < rows * lanes:
            r, l = divmod(i, lanes)
            out[place] = src[r * 16 : r * 16 + 16, l * 128 : l * 128 + 128].astype(BF16)
        else:
            out[place] = jnp.zeros((16, 128), BF16)


def all_in(held, sem, place):
    remote(held, held, sem, sem, place).wait_recv()


def all_out(held, sem, place):
    remote(held, held, sem, sem, place).wait_send()


def tile_sum(a, b):
    return a.astype(F32) + b.astype(F32)


class Bound:
    def shapes(self):
        raise NotImplementedError

    def scratch(self):
        shapes = self.shapes()
        self.names = list(shapes)
        return list(shapes.values())

    def bind(self, spot, refs):
        self.spot = spot
        for name, ref in zip(self.names, refs):
            setattr(self, name, ref)


class OverZ(Bound):
    def z_shapes(self, lines, nz):
        sem = pltpu.SemaphoreType.DMA
        self.zlen = lines // nz
        self.zpad = up_to(self.zlen, 16)
        piece = (nz, self.zpad, 128)
        return dict(
            rows=pltpu.VMEM((lines, 128), F32), zrows=pltpu.VMEM(piece, F32),
            zsend=pltpu.VMEM(piece, BF16), zrecv=pltpu.VMEM(piece, BF16), zall=pltpu.VMEM(piece, BF16),
            z1s=sem((1,)), z1r=sem((1,)), z2s=sem((1,)), z2r=sem((1,)),
        )

    def z_send_rows(self):
        s, n = self.spot, self.zlen
        if n < self.zpad:
            self.zrows[...] = jnp.zeros_like(self.zrows)
        for i in range(s.nz):
            self.zrows[i, :n, :] = self.rows[i * n : (i + 1) * n, :]
        self.zsend[...] = self.zrows[...].astype(BF16)

        def send(d):
            p = s.z_peer(d)
            remote(self.zsend.at[p], self.zrecv.at[d], self.z1s.at[0], self.z1r.at[0], s.at_z(p)).start()

        each(1, s.nz, send)

    def z_back(self):
        s = self.spot
        rest = pl.ds(1, s.nz - 1)
        all_in(self.zrecv.at[rest], self.z1r.at[0], s.other)
        total = self.zsend[s.z].astype(F32)
        for d in range(1, s.nz):
            total = total + self.zrecv[d].astype(F32)
        self.zall[s.z] = total.astype(BF16)
        mine = self.zall.at[s.z]
        each(1, s.nz, lambda d: remote(mine, mine, self.z2s.at[0], self.z2r.at[0], s.at_z(s.z_peer(d))).start())

    def z_take_rows(self):
        s, n = self.spot, self.zlen
        rest = pl.ds(1, s.nz - 1)
        all_in(self.zall.at[rest], self.z2r.at[0], s.other)
        self.zrows[...] = self.zall[...].astype(F32)
        for i in range(s.nz):
            self.rows[i * n : (i + 1) * n, :] = self.zrows[i, :n, :]

    def z_drain(self):
        rest = pl.ds(1, self.spot.nz - 1)
        all_out(self.zsend.at[rest], self.z1s.at[0], self.spot.other)
        all_out(self.zall.at[rest], self.z2s.at[0], self.spot.other)


class WeightSum(OverZ):
    def __init__(self, plan, columns, whole):
        self.plan, self.columns, self.whole = plan, columns, whole
        self.wt = plan.weight_tiles(columns)

    def out_shape(self):
        return jax.ShapeDtypeStruct((2, self.plan.plane, self.wt, 16, 128), BF16)

    def shapes(self):
        plane, nz, wt = self.plan.plane, self.plan.nz, self.wt
        sem = pltpu.SemaphoreType.DMA
        full, half = (2, plane, wt, 16, 128), (plane, wt, 16, 128)
        shapes = dict(
            wsend=pltpu.VMEM(full, BF16), wr1=pltpu.VMEM(half, BF16), w1=pltpu.VMEM(half, BF16),
            wr2=pltpu.VMEM(half, BF16), wall=pltpu.VMEM(full, BF16),
            c1s=sem((1,)), c1r=sem((1,)), p2s=sem((1,)), p2r=sem((1,)),
            p3s=sem((1,)), p3r=sem((1,)), c4s=sem((1,)), c4r=sem((1,)),
        )
        if self.whole:
            shapes.update(zrecv=pltpu.VMEM((nz, wt, 16, 128), BF16), z1s=sem((1,)), z1r=sem((1,)))
        else:
            shapes.update(self.z_shapes(wt * 16, nz))
        return shapes

    def core_copy(self):
        s = self.spot
        return remote(self.wsend.at[1 - s.core], self.wr1, self.c1s.at[0], self.c1r.at[0], s.other)

    def hand(self):
        s = self.spot
        held = self.wall.at[s.core]
        return remote(held, held, self.c4s.at[0], self.c4r.at[0], s.other)

    def fill(self, total):
        cut(total, self.wsend, self.columns // 128, C // 16, self.plan.plane, self.wt)

    def core_start(self):
        self.core_copy().start()

    def plane_start(self):
        s = self.spot
        self.core_copy().wait_recv()
        self.w1[...] = tile_sum(self.wsend[s.core], self.wr1[...]).astype(BF16)

        def send(d):
            p = s.plane_peer(d)
            remote(self.w1.at[p], self.wr2.at[d], self.p2s.at[0], self.p2r.at[0], s.at_plane(p)).start()

        each(1, s.plane, send)

    def z_start(self):
        s = self.spot
        all_in(self.wr2.at[pl.ds(1, s.plane - 1)], self.p2r.at[0], s.other)
        total = tile_sum(self.wsend[s.core, s.me], self.wr1[s.me])
        for d in range(1, s.plane):
            total = total + self.wr2[d].astype(F32)
        if self.whole:
            self.zrecv[s.z] = total.astype(BF16)
            mine = self.zrecv.at[s.z]
            each(1, s.nz, lambda d: remote(mine, mine, self.z1s.at[0], self.z1r.at[0], s.at_z(s.z_peer(d))).start())
        else:
            self.rows[...] = total.reshape(self.wt * 16, 128)
            self.z_send_rows()

    def plane_back(self):
        s = self.spot
        if self.whole:
            all_in(self.zrecv.at[pl.ds(1, s.nz - 1)], self.z1r.at[0], s.other)
            total = self.zrecv[0].astype(F32)
            for i in range(1, s.nz):
                total = total + self.zrecv[i].astype(F32)
        else:
            self.z_take_rows()
            total = self.rows[...].reshape(self.wt, 16, 128)
        self.wall[s.core, s.me] = total.astype(BF16)
        mine = self.wall.at[s.core, s.me]
        each(
            1, s.plane,
            lambda d: remote(mine, mine, self.p3s.at[0], self.p3r.at[0], s.at_plane(s.plane_peer(d))).start(),
        )

    def hand_over(self):
        s = self.spot
        all_in(self.wall.at[s.core, pl.ds(1, s.plane - 1)], self.p3r.at[0], s.other)
        self.hand().start()

    def finish(self):
        self.hand().wait_recv()

    def drain(self):
        s = self.spot
        rest = pl.ds(1, s.plane - 1)
        self.core_copy().wait_send()
        all_out(self.w1.at[rest], self.p2s.at[0], s.other)
        all_out(self.wall.at[s.core, rest], self.p3s.at[0], s.other)
        if self.whole:
            all_out(self.zrecv.at[pl.ds(1, s.nz - 1)], self.z1s.at[0], s.other)
        else:
            self.z_drain()
        self.hand().wait_send()


class TableSum(OverZ):
    def __init__(self, plan):
        self.plan = plan

    def out_shape(self):
        return jax.ShapeDtypeStruct((2, XL, self.plan.tt, 16, 128), BF16)

    def shapes(self):
        tt, nz = self.plan.tt, self.plan.nz
        sem = pltpu.SemaphoreType.DMA
        full, half, part = (2, XL, tt, 16, 128), (XL, tt, 16, 128), (tt, 16, 128)
        shapes = dict(
            tsend=pltpu.VMEM(full, BF16), tr1=pltpu.VMEM(half, BF16), t1=pltpu.VMEM(part, BF16),
            tr2=pltpu.VMEM(part, BF16), wall=pltpu.VMEM(full, BF16),
            send=sem((5,)), recv=sem((5,)),
        )
        shapes.update(self.z_shapes(tt * 16, nz))
        return shapes

    def copies(self, n):
        s = self.spot
        if n == 0:
            src, dst, place = self.tsend.at[1 - s.core], self.tr1, s.other
        elif n == 1:
            src, dst, place = self.t1, self.tr2, s.across
        else:
            src = dst = self.wall.at[s.core, 1 - s.xl if n == 4 else s.xl]
            place = s.across if n == 2 else s.other
        return remote(src, dst, self.send.at[n], self.recv.at[n], place)

    def fill(self, total):
        cut(total, self.tsend, TLANES, TROWS // 16, XL, self.plan.tt)

    def core_start(self):
        self.copies(0).start()

    def pair_start(self):
        s = self.spot
        self.copies(0).wait_recv()
        far = 1 - s.xl
        self.t1[...] = tile_sum(self.tsend[s.core, far], self.tr1[far]).astype(BF16)
        self.copies(1).start()

    def z_start(self):
        s = self.spot
        near = tile_sum(self.tsend[s.core, s.xl], self.tr1[s.xl])
        self.copies(1).wait_recv()
        self.rows[...] = (near + self.tr2[...].astype(F32)).reshape(self.plan.tt * 16, 128)
        self.z_send_rows()

    def pair_back(self):
        s = self.spot
        self.z_take_rows()
        self.wall[s.core, s.xl] = self.rows[...].astype(BF16).reshape(self.plan.tt, 16, 128)
        self.copies(2).start()
        self.copies(3).start()

    def hand_over(self):
        self.copies(2).wait_recv()
        self.copies(4).start()

    def finish(self):
        self.copies(3).wait_recv()
        self.copies(4).wait_recv()

    def drain(self):
        for n in range(5):
            self.copies(n).wait_send()
        self.z_drain()


def normed_of(v):
    centred = v - jnp.mean(v, axis=-1, keepdims=True)
    inv = lax.rsqrt(jnp.mean(centred * centred, axis=-1, keepdims=True) + NORM_EPS)
    return centred * inv, inv


def norm_back(up, normed, inv):
    return inv * (
        up
        - jnp.mean(up, axis=-1, keepdims=True)
        - normed * jnp.mean(up * normed, axis=-1, keepdims=True)
    )


FAR = (
    "w_qkv", "w_proj", "w_up", "w_downt", "order", "back",
    "even_lane", "odd_lane", "tsum", "ccol",
)
LANES = ("even_lane", "odd_lane")
QUARTERS = (4, QUARTER + EXTRA, PACK)
SCRATCH = dict(
    packed=(QUARTERS, F32),
    outward=(QUARTERS, BF16),
    frame=(QUARTERS, BF16),
    tn=((TLANES, TROWS, 128), F32),
    lined=((2, TROWS, KCOLS), F32),
    spread=((2 * TROWS, KCOLS), F32),
    bars=((2, WIN, WIN), F32),
    xs=((CELLS, C), F32),
    gm=((CELLS, C), BF16),
    act=((CELLS, C), BF16),
    q=((CELLS, C), BF16),
    k=((CELLS, C), BF16),
    v=((CELLS, C), BF16),
    qkvt=((NWIN, 3 * C, WIN), BF16),
    ot=((NWIN, C, WIN), BF16),
    dot=((NWIN, C, WIN), BF16),
    dh=((CELLS, C), BF16),
    dout=((CELLS, C), BF16),
    b=((CELLS, C), BF16),
    m=((CELLS, MLP), BF16),
    du=((CELLS, MLP), BF16),
    dqkvt=((3 * C, WIN), BF16),
    back=((CELLS, C), F32),
    wqkvt=((3 * C, C), BF16),
    bias=((NWIN * HEADS, WIN, WIN), F32),
    prob=((NWIN * HEADS, WIN, WIN), F32),
    probb=((NWIN * HEADS, WIN, WIN), BF16),
    dcol=((PAIRS, 2 * TROWS, WIN), F32),
    early=((C, ECOLS), F32),
    late=((C, LCOLS), F32),
    lsum=((3 * C, C), F32),
    tgrad=((TROWS, TLANES * 128), F32),
    send=((4, QUARTER, C), BF16),
    hrecv=((4, QUARTER, C), BF16),
)


def block_kernel(plan, sums, *refs):
    x_ref, g_ref, valid_ref, slab_ref, table_ref = refs[:5]
    far = refs[5 : 5 + len(FAR)]
    refs = refs[5 + len(FAR) :]
    home_ref, early_ref, late_ref, tall_ref = refs[:4]
    near = dict(zip(FAR, refs[4 : 4 + len(FAR)]))
    refs = refs[4 + len(FAR) :]
    s = dict(zip(SCRATCH, refs))
    refs = refs[len(SCRATCH) :]
    fs, es, er, hs, hr, outs = refs[:6]
    refs = refs[6:]
    spot = Spot(plan)
    early, late, table = sums
    for one in sums:
        one.bind(spot, refs[: len(one.names)])
        refs = refs[len(one.names) :]
    before, after = neighbours(plan)
    for place in before + after:
        greet(place)
    greeted = spot.greet_all() + 6
    fetch = [pltpu.make_async_copy(src, near[name], fs.at[n]) for n, (name, src) in enumerate(zip(FAR, far))]
    for copy in fetch:
        copy.start()
    w_qkv, w_proj, w_up, w_downt, order_ref, back_ref, tsum_ref, ccol_ref = (
        near[n] for n in ("w_qkv", "w_proj", "w_up", "w_downt", "order", "back", "tsum", "ccol")
    )

    hm = []
    lane = lax.broadcasted_iota(jnp.int32, (1, C), 1)
    for h in range(HEADS):
        hm.append(jnp.where(lane // HEAD_DIM == h, 1.0, 0.0).astype(BF16))
    scale = HEAD_DIM ** (-0.5)

    slab = slab_ref[...]
    packed, outward, frame = s["packed"], s["outward"], s["frame"]
    packed[:, QUARTER:, :] = jnp.zeros((4, EXTRA, PACK), F32)
    for part, ref in enumerate((x_ref, g_ref)):
        rows = dot(slab, ref[...])
        for c in range(WW):
            for rs in range(2):
                piece = rows[rs * SLAB : (rs + 1) * SLAB, c * C : (c + 1) * C]
                if part == 1:
                    piece = piece * valid_ref[0, c].astype(F32)
                packed[
                    rs * 2 + c // CH, (c % CH) * SLAB : (c % CH + 1) * SLAB, part * C : (part + 1) * C
                ] = piece
    for c in range(WW):
        mark = jnp.full((1, PACK), valid_ref[0, c].astype(F32), F32)
        for rs in range(2):
            packed[rs * 2 + c // CH, QUARTER + c % CH : QUARTER + c % CH + 1, :] = mark
    outward[...] = packed[...].astype(BF16)
    blank = jnp.zeros((NWIN, TLANES * 128 - TCOLS), F32)
    for h in range(HEADS):
        for zi in range(WZ):
            for ri in range(WH):
                pieces = [table_ref[:, at : at + TSEG] for at in segments(h, zi, ri)]
                line = jnp.concatenate(pieces + [blank], axis=1)
                rows = pl.ds(h * ZR + zi * WH + ri, NWIN, stride=HEADS * ZR)
                for l in range(TLANES):
                    s["tn"][l, rows, :] = line[:, l * 128 : (l + 1) * 128]
    pl.semaphore_wait(pltpu.get_barrier_semaphore(), greeted)
    enter = [
        remote(outward.at[2], frame.at[1], es.at[0], er.at[0], before[0]),
        remote(outward.at[1], frame.at[2], es.at[1], er.at[1], before[1]),
        remote(outward.at[0], frame.at[3], es.at[2], er.at[2], before[2]),
    ]
    for copy in enter:
        copy.start()
    frame[0] = outward[3]

    for copy in fetch:
        copy.wait()
    left = jnp.concatenate([s["tn"][l] for l in range(TLANES)], axis=1)[:, :TCOLS]
    for n in range(3):
        term = left.astype(BF16)
        left = left - term.astype(F32)
        for odd in range(2):
            part = dot(term, near[LANES[odd]][...])
            if n == 0:
                s["lined"][odd] = part
            else:
                s["lined"][odd] += part
    for i in range(NWIN * HEADS):
        for odd in range(2):
            s["spread"][i * STRIP + odd * ZR : i * STRIP + (odd + 1) * ZR, :] = s["lined"][
                odd, i * ZR : (i + 1) * ZR, :
            ]
    for t in range(NWIN):
        for pair in range(PAIRS):
            first = (WW - 1 - 2 * pair) * ZR
            rows = s["spread"][t * HEADS * STRIP : (t + 1) * HEADS * STRIP, first : first + WIN]
            s["bias"][t * HEADS : (t + 1) * HEADS, pair * STRIP : (pair + 1) * STRIP, :] = rows.reshape(
                HEADS, STRIP, WIN
            )
    s["wqkvt"][...] = w_qkv[...].T
    ccol = ccol_ref[...]
    ii = lax.broadcasted_iota(jnp.int32, (WIN, WIN), 0)
    jj = lax.broadcasted_iota(jnp.int32, (WIN, WIN), 1)
    low_i, low_j = (lax.rem(ii, WH) >= RH).astype(jnp.int32), (lax.rem(jj, WH) >= RH).astype(jnp.int32)
    open_rows = jnp.where(lax.axis_index("lat") == plan.lat - 1, 0, 1)
    top_i, top_j = lax.rem(ii // WH, WZ), lax.rem(jj // WH, WZ)
    s["bars"][0] = jnp.where((low_i == low_j) | (open_rows == 1), 0.0, MASKED)
    s["bars"][1] = jnp.where(top_i == top_j, 0.0, MASKED)
    for copy in enter:
        copy.wait_recv()

    cells = dot(order_ref[...], frame[:, :QUARTER, :].reshape(CELLS, PACK))
    s["xs"][...] = cells[:, :C]
    s["gm"][...] = cells[:, C:].astype(BF16)

    marks = jnp.concatenate(
        [
            frame[0, QUARTER : QUARTER + EXTRA, :WIN][:CH].astype(F32),
            frame[1, QUARTER : QUARTER + EXTRA, :WIN][:CH].astype(F32),
            jnp.zeros((EXTRA - WW, WIN), F32),
        ],
        axis=0,
    ).astype(BF16)
    same = dot(ccol, marks) == lax.dot_general(
        marks, ccol, (((0,), (1,)), ((), ())), preferred_element_type=F32
    )
    barred = jnp.where(same, s["bars"][0], MASKED)
    s["bars"][0] = barred
    s["bars"][1] = jnp.minimum(barred, s["bars"][1])

    normed, inv = normed_of(s["xs"][...])
    a = normed.astype(BF16)
    s["act"][...] = a
    s["q"][...] = dot(a, w_qkv[:, :C]).astype(BF16)
    s["k"][...] = dot(a, w_qkv[:, C : 2 * C]).astype(BF16)
    s["v"][...] = dot(a, w_qkv[:, 2 * C :]).astype(BF16)

    def forward(w, carry):
        at = pl.ds(pl.multiple_of(w * WIN, WIN), WIN)
        q, k = s["q"][at, :], s["k"][at, :]
        bar = s["bars"][(w == NWIN - 1).astype(jnp.int32)]
        qkvt = dot_nt(s["wqkvt"][...], s["act"][at, :]).astype(BF16)
        s["qkvt"][w] = qkvt
        heads = pl.ds(w * HEADS, HEADS)
        split = jnp.concatenate([q * hm[h] for h in range(HEADS)], axis=0)
        score = dot_nt(split, k).reshape(HEADS, WIN, WIN) * scale + s["bias"][heads] + bar
        e = jnp.exp(score - jnp.max(score, axis=-1, keepdims=True))
        p = e * (1.0 / jnp.sum(e, axis=-1, keepdims=True))
        s["prob"][heads] = p
        pb = p.astype(BF16)
        s["probb"][heads] = pb
        for h in range(HEADS):
            head = 2 * C + h * HEAD_DIM
            s["ot"][w, h * HEAD_DIM : (h + 1) * HEAD_DIM, :] = dot_nt(
                qkvt[head : head + HEAD_DIM, :], pb[h]
            ).astype(BF16)
        return carry

    lax.fori_loop(0, NWIN, forward, 0)

    mixed = jnp.concatenate([dot_tn(s["ot"][w], w_proj[...]) for w in range(NWIN)], axis=0)
    mid = (s["xs"][...] + mixed).astype(BF16).astype(F32)
    n2, inv2 = normed_of(mid)
    b = n2.astype(BF16)
    s["b"][...] = b
    u = dot(b, w_up[...])
    cdf = 0.5 * (1.0 + lax.erf(u * 0.7071067811865476))
    s["m"][...] = (u * cdf).astype(BF16)
    slope = cdf + u * jnp.exp(-0.5 * u * u) * 0.3989422804014327
    g = s["gm"][...]
    du = (dot(g, w_downt[...]) * slope).astype(BF16)
    s["du"][...] = du
    dh = (g.astype(F32) + norm_back(dot_nt(du, w_up[...]), n2, inv2)).astype(BF16)
    s["dh"][...] = dh
    s["dout"][...] = dot_nt(dh, w_proj[...]).astype(BF16)
    for w in range(NWIN):
        s["dot"][w] = dot_nt(w_proj[...], dh[w * WIN : (w + 1) * WIN, :]).astype(BF16)
    s["early"][:, :MLP] = dot_tn(s["b"][...], s["du"][...])
    s["early"][:, MLP:] = dot_tn(s["gm"][...], s["m"][:, :DOWN])
    early.fill(s["early"])
    early.core_start()

    for w in range(NWIN):
        at = pl.ds(w * WIN, WIN)
        k, v, do = s["k"][at, :], s["v"][at, :], s["dout"][at, :]
        split = jnp.concatenate([do * hm[h] for h in range(HEADS)], axis=0)
        dp = dot_nt(split, v).reshape(HEADS, WIN, WIN)
        p = s["prob"][w * HEADS : (w + 1) * HEADS]
        ds = p * (dp - jnp.sum(p * dp, axis=-1, keepdims=True))
        dsb = ds.astype(BF16)
        for h in range(HEADS):
            first = (w * HEADS + h) * STRIP
            for pair in range(PAIRS):
                s["dcol"][pair, first : first + STRIP, :] = ds[h, pair * STRIP : (pair + 1) * STRIP, :]
            low, high = h * HEAD_DIM, (h + 1) * HEAD_DIM
            kt, qt = s["qkvt"][w, C + low : C + high, :], s["qkvt"][w, low:high, :]
            s["dqkvt"][low:high, :] = (dot_nt(kt, dsb[h]) * scale).astype(BF16)
            s["dqkvt"][C + low : C + high, :] = (dot(qt, dsb[h]) * scale).astype(BF16)
            s["dqkvt"][2 * C + low : 2 * C + high, :] = dot(
                s["dot"][w, low:high, :], s["probb"][w * HEADS + h]
            ).astype(BF16)
        dqkvt = s["dqkvt"][...]
        s["back"][at, :] = dot(w_qkv[...], dqkvt).T
        term = dot(dqkvt, s["act"][at, :])
        if w == 0:
            s["lsum"][...] = term
        else:
            s["lsum"][...] += term
        if w == NWIN - 2:
            early.plane_start()

    grad = jnp.zeros((2 * TROWS, KCOLS), F32)
    for pair in range(PAIRS):
        grad += dot(s["dcol"][pair].astype(BF16), tsum_ref[pair])
    s["spread"][...] = grad
    for i in range(NWIN * HEADS):
        for odd in range(2):
            s["lined"][odd, i * ZR : (i + 1) * ZR, :] = s["spread"][
                i * STRIP + odd * ZR : i * STRIP + (odd + 1) * ZR, :
            ]
    s["tgrad"][:, TCOLS:] = jnp.zeros((TROWS, TLANES * 128 - TCOLS), F32)
    s["tgrad"][:, :TCOLS] = dot_nt(s["lined"][0].astype(BF16), near["even_lane"][...]) + dot_nt(
        s["lined"][1].astype(BF16), near["odd_lane"][...]
    )
    table.fill(s["tgrad"])
    table.core_start()
    s["late"][:, : 3 * C] = s["lsum"][...].T
    proj = jnp.zeros((C, C), F32)
    for w in range(NWIN):
        proj += dot(s["ot"][w], s["dh"][w * WIN : (w + 1) * WIN, :])
    s["late"][:, 3 * C : 4 * C] = proj
    s["late"][:, 4 * C :] = dot_tn(s["gm"][...], s["m"][:, DOWN:])
    late.fill(s["late"])
    late.core_start()

    normed, inv = normed_of(s["xs"][...])
    dxs = (s["dh"][...].astype(F32) + norm_back(s["back"][...], normed, inv)).astype(BF16)
    s["send"][...] = dot(back_ref[...], dxs).astype(BF16).reshape(4, QUARTER, C)
    home = [
        remote(s["send"].at[1], s["hrecv"].at[2], hs.at[0], hr.at[0], after[0]),
        remote(s["send"].at[2], s["hrecv"].at[1], hs.at[1], hr.at[1], after[1]),
        remote(s["send"].at[3], s["hrecv"].at[0], hs.at[2], hr.at[2], after[2]),
    ]
    table.pair_start()
    late.plane_start()
    for copy in home:
        copy.start()
    home_ref[3] = s["send"][0]

    early.z_start()
    table.z_start()
    late.z_start()
    early.z_back()
    table.z_back()
    early.plane_back()
    table.pair_back()
    late.plane_back()
    table.hand_over()
    for copy in home:
        copy.wait_recv()
    for q in range(3):
        home_ref[q] = s["hrecv"][q]
    early.hand_over()
    late.hand_over()
    leave = []
    for n, (one, out) in enumerate(((table, tall_ref), (early, early_ref), (late, late_ref))):
        one.finish()
        leave.append(pltpu.make_async_copy(one.wall, out, outs.at[n]))
        leave[-1].start()
    for copy in enter + home:
        copy.wait_send()
    for one in sums:
        one.drain()
    for copy in leave:
        copy.wait()


def block(plan, state, cotangent, valid, table, w_qkv, w_proj, w_up, w_down):
    vmem = pl.BlockSpec(memory_space=pltpu.VMEM)
    hbm = pl.BlockSpec(memory_space=pl.ANY)
    order = cell_order()
    sums = (WeightSum(plan, ECOLS, False), WeightSum(plan, LCOLS, True), TableSum(plan))
    consts = (
        order, order.T, table_lanes(0), table_lanes(1), table_sums(), column_of_cell(),
    )
    far = [w_qkv, w_proj, w_up, w_down.T] + [jnp.asarray(m, BF16) for m in consts]
    scratch = [pltpu.VMEM(v.shape, v.dtype) for v in far]
    scratch += [pltpu.VMEM(shape, dtype) for shape, dtype in SCRATCH.values()]
    sem = pltpu.SemaphoreType.DMA
    scratch += [sem((len(FAR),)), sem((3,)), sem((3,)), sem((3,)), sem((3,)), sem((3,))]
    for one in sums:
        scratch += one.scratch()
    rows = lambda v: v.transpose(1, 0, 2).reshape(WH * LEVELS, WW * C)
    return pl.pallas_call(
        functools.partial(block_kernel, plan, sums),
        out_shape=[jax.ShapeDtypeStruct((4, QUARTER, C), BF16)] + [one.out_shape() for one in sums],
        in_specs=[vmem, vmem, pl.BlockSpec(memory_space=pltpu.SMEM), vmem, vmem] + [hbm] * len(far),
        out_specs=[vmem, hbm, hbm, hbm],
        scratch_shapes=scratch,
        compiler_params=pltpu.CompilerParams(
            collective_id=0, has_side_effects=True, vmem_limit_bytes=VMEM_LIMIT
        ),
        name="block",
    )(
        rows(state), rows(cotangent), valid.reshape(1, WW), jnp.asarray(slab_order(), BF16), table, *far
    )


def write_kernel(
    plan, factor, home_ref, early_ref, late_ref, tall_ref, slab_ref,
    dx_ref, qkv_ref, proj_ref, up_ref, down_ref, table_ref, band, early, late, tgrad,
):
    jobs = (
        (early_ref, early, ECOLS // 128, C // 16, plan.plane, factor),
        (late_ref, late, LCOLS // 128, C // 16, plan.plane, factor),
        (tall_ref, tgrad, TLANES, TROWS // 16, XL, 1.0),
    )
    for src, dst, lanes, rows, parts, gain in jobs:
        tiles = src.shape[2]
        for i in range(rows * lanes):
            core, rest = divmod(i, parts * tiles)
            r, l = divmod(i, lanes)
            value = src[core, rest // tiles, rest % tiles].astype(F32)
            if dst is tgrad:
                dst[l, r * 16 : r * 16 + 16, :] = value
            else:
                dst[r * 16 : r * 16 + 16, l * 128 : l * 128 + 128] = value * gain
    up_ref[...] = early[:, :MLP]
    down_ref[:, :DOWN] = early[:, MLP:]
    down_ref[:, DOWN:] = late[:, 4 * C :]
    proj_ref[...] = late[:, 3 * C : 4 * C]
    qkv_ref[...] = late[:, : 3 * C]
    for h in range(HEADS):
        for zi in range(WZ):
            for ri in range(WH):
                rows = pl.ds(h * ZR + zi * WH + ri, NWIN, stride=HEADS * ZR)
                line = jnp.concatenate(
                    [tgrad[l, rows, :] for l in range(TLANES)], axis=1
                )
                for zj, at in enumerate(segments(h, zi, ri)):
                    table_ref[:, at : at + TSEG] = line[:, zj * TSEG : (zj + 1) * TSEG]
    for c in range(WW):
        for rs in range(2):
            band[rs * SLAB : (rs + 1) * SLAB, c * C : (c + 1) * C] = home_ref[
                rs * 2 + c // CH, (c % CH) * SLAB : (c % CH + 1) * SLAB, :
            ].astype(F32)
    dx_ref[...] = dot(slab_ref[...], band[...].astype(BF16)).astype(BF16)


def write(plan, home, early, late, tall):
    vmem = pl.BlockSpec(memory_space=pltpu.VMEM)
    factor = float(CELLS * plan.lon * plan.lat) ** (-0.5)
    dx, qkv, proj, up, down, table = pl.pallas_call(
        functools.partial(write_kernel, plan, factor),
        out_shape=(
            jax.ShapeDtypeStruct((WH * LEVELS, WW * C), BF16),
            jax.ShapeDtypeStruct((C, 3 * C), F32),
            jax.ShapeDtypeStruct((C, C), F32),
            jax.ShapeDtypeStruct((C, MLP), F32),
            jax.ShapeDtypeStruct((C, MLP), F32),
            jax.ShapeDtypeStruct((NWIN, HEADS * ZR * ZR * SPAN), F32),
        ),
        in_specs=[vmem] * 5,
        out_specs=(vmem,) * 6,
        scratch_shapes=[
            pltpu.VMEM((2 * SLAB, WW * C), F32),
            pltpu.VMEM((C, ECOLS), F32),
            pltpu.VMEM((C, LCOLS), F32),
            pltpu.VMEM((TLANES, TROWS, 128), F32),
        ],
        compiler_params=pltpu.CompilerParams(vmem_limit_bytes=VMEM_LIMIT),
        name="write",
    )(home, early, late, tall, jnp.asarray(slab_order().T, BF16))
    dx = dx.reshape(WH, LEVELS, WW * C).transpose(1, 0, 2)
    return dx, qkv, proj, up, down.T, table


def per_device(plan, state_in, cotangent, w_qkv, w_proj, w_up, w_down, bias_table, pad_valid):
    return write(plan, *block(plan, state_in, cotangent, pad_valid, bias_table, w_qkv, w_proj, w_up, w_down))


def solution(mesh):
    plan = Plan(mesh.shape["lon"], mesh.shape["lat"])
    return jax.shard_map(
        functools.partial(per_device, plan),
        mesh=mesh,
        in_specs=(
            P(None, "lat", "lon"),
            P(None, "lat", "lon"),
            P(),
            P(),
            P(),
            P(),
            P("lat", None),
            P("lon"),
        ),
        out_specs=(P(None, "lat", "lon"), P(), P(), P(), P(), P("lat", None)),
        check_vma=False,
    )
```

time: 90.4 us -> 80.6 us (0.89)
  Pallas kernels: 89.6 us -> 79.7 us
    pallas_call x1, Pallas kernels: 86.5 us -> 76.7 us  [block(): pl.pallas_call(functools.partial(block_kernel, plan, sums), out_shape=[ja...]
where the time goes in v3:
time: 80.6 us; the launch traced here: 80.4 us
  Pallas kernels  79.7 us (99%)
    pallas_call x1, Pallas kernels, block(): pl.pallas_call(functools.partial(block_kernel, plan, sums), out_shape=[ja...  76.7 us
    pallas_call x1, Pallas kernels, write(): pl.pallas_call(functools.partial(write_kernel, plan, factor), out_shape=(...  3.05 us

profile of v3, /device:TPU:1, one launch (start us, length us, event | category | flops | bytes accessed | tf_op | source)
XLA Modules:
  0.0 80.4 jit_solution(17209003656139364603)
XLA Ops:
  0.6 76.7 %block.1 = (bf16[4,144,192]{2,1,0:T(8,128)(2,1)}, bf16[2,16,4,16,128]{4,3,2,1,0:T(8,128)(2,1)}, bf16[2,16,3,16,128]{4,3,2,1,0:T(8,128)(2,1)}, bf16[2,2,14,16,128]{4,3,2,1,0:T(8,128)(2,1)}) custom-call(bf16[48,2304]{1,0:T(8,128)(2,1)} %bitcast.13, bf16[48,2304]{1,0:T(8,128)(2,1)} %bitcast.14, s32[1,12]{1,0:T(1,128)} %bitcast.15, ...), custom_call_target="tpu_custom_call" | custom-call | tf_op jit(solution)/shard_map/block/pallas_call | solution.py:808
  77.3 3.1 %write.1 = (bf16[48,2304]{1,0:T(8,128)(2,1)}, f32[192,576]{1,0:T(8,128)}, f32[192,192]{1,0:T(8,128)}, f32[192,768]{1,0:T(8,128)}, f32[192,768]{1,0:T(8,128)}, /*index=5*/f32[4,19872]{1,0:T(4,128)}) custom-call(bf16[4,144,192]{2,1,0:T(8,128)(2,1)} %get-tuple-element.16.home_ref, bf16[2,16,4,16,128]{4,3,2,1,0:T(8,128)(2,1)} %get-tuple-element.17.early_ref, ...), custom_call_target="tpu_custom_call" | custom-call | tf_op jit(solution)/shard_map/write/pallas_call | solution.py:867

commit v4 on v3

--- a/solution.py
+++ b/solution.py
@@ -172,27 +172,30 @@
         self.z = lax.rem(self.lon // 2, self.nz)
         self.xl = self.lon // (2 * self.nz)
         self.me = self.xl * plan.lat + self.lat
-        self.other = self.at(self.me, self.z, 1 - self.core)
-        self.across = self.at((1 - self.xl) * plan.lat + self.lat, self.z, self.core)
-
-    def at(self, p, z, core):
-        return (p // self.plan.lat) * (2 * self.nz) + z * 2 + core, lax.rem(p, self.plan.lat)
-
-    def at_plane(self, p):
-        return self.at(p, self.z, self.core)
+        self.other = self.at(self.xl, self.lat, self.z, 1 - self.core)
+        self.across = self.at(1 - self.xl, self.lat, self.z, self.core)
+
+    def at(self, xl, lat, z, core):
+        return xl * (2 * self.nz) + z * 2 + core, lat
 
     def at_z(self, z):
-        return self.at(self.me, z, self.core)
+        return self.at(self.xl, self.lat, z, self.core)
 
     def plane_peer(self, d):
-        return lax.rem(self.me + d, self.plane)
+        rows = self.plan.lat
+        far = (d >= rows).astype(jnp.int32)
+        lat = self.lat + d - far * rows
+        lat = lat - rows * (lat >= rows).astype(jnp.int32)
+        xl = self.xl + far - 2 * self.xl * far
+        return xl * rows + lat, self.at(xl, lat, self.z, self.core)
 
     def z_peer(self, d):
-        return lax.rem(self.z + d, self.nz)
+        z = self.z + d
+        return z - self.nz * (z >= self.nz).astype(jnp.int32)
 
     def greet_all(self):
         greet(self.other)
-        each(1, self.plane, lambda d: greet(self.at_plane(self.plane_peer(d))))
+        each(1, self.plane, lambda d: greet(self.plane_peer(d)[1]))
         each(1, self.nz, lambda d: greet(self.at_z(self.z_peer(d))))
         return 1 + self.plane - 1 + self.nz - 1
 
@@ -331,8 +334,8 @@
         self.w1[...] = tile_sum(self.wsend[s.core], self.wr1[...]).astype(BF16)
 
         def send(d):
-            p = s.plane_peer(d)
-            remote(self.w1.at[p], self.wr2.at[d], self.p2s.at[0], self.p2r.at[0], s.at_plane(p)).start()
+            p, place = s.plane_peer(d)
+            remote(self.w1.at[p], self.wr2.at[d], self.p2s.at[0], self.p2r.at[0], place).start()
 
         each(1, s.plane, send)
 
@@ -364,7 +367,7 @@
         mine = self.wall.at[s.core, s.me]
         each(
             1, s.plane,
-            lambda d: remote(mine, mine, self.p3s.at[0], self.p3r.at[0], s.at_plane(s.plane_peer(d))).start(),
+            lambda d: remote(mine, mine, self.p3s.at[0], self.p3r.at[0], s.plane_peer(d)[1]).start(),
         )
 
     def hand_over(self):
@@ -568,6 +571,18 @@
         for rs in range(2):
             packed[rs * 2 + c // CH, QUARTER + c % CH : QUARTER + c % CH + 1, :] = mark
     outward[...] = packed[...].astype(BF16)
+    pl.semaphore_wait(pltpu.get_barrier_semaphore(), greeted)
+    enter = []
+    for lanes in (pl.ds(0, 2 * 128), pl.ds(2 * 128, 128)):
+        for out, into, place in zip((2, 1, 0), (1, 2, 3), before):
+            n = len(enter)
+            enter.append(
+                remote(outward.at[out, :, lanes], frame.at[into, :, lanes], es.at[n], er.at[n], place)
+            )
+    for copy in enter:
+        copy.start()
+    frame[0] = outward[3]
+
     blank = jnp.zeros((NWIN, TLANES * 128 - TCOLS), F32)
     for h in range(HEADS):
         for zi in range(WZ):
@@ -577,16 +592,6 @@
                 rows = pl.ds(h * ZR + zi * WH + ri, NWIN, stride=HEADS * ZR)
                 for l in range(TLANES):
                     s["tn"][l, rows, :] = line[:, l * 128 : (l + 1) * 128]
-    pl.semaphore_wait(pltpu.get_barrier_semaphore(), greeted)
-    enter = [
-        remote(outward.at[2], frame.at[1], es.at[0], er.at[0], before[0]),
-        remote(outward.at[1], frame.at[2], es.at[1], er.at[1], before[1]),
-        remote(outward.at[0], frame.at[3], es.at[2], er.at[2], before[2]),
-    ]
-    for copy in enter:
-        copy.start()
-    frame[0] = outward[3]
-
     for copy in fetch:
         copy.wait()
     left = jnp.concatenate([s["tn"][l] for l in range(TLANES)], axis=1)[:, :TCOLS]
@@ -620,12 +625,10 @@
     top_i, top_j = lax.rem(ii // WH, WZ), lax.rem(jj // WH, WZ)
     s["bars"][0] = jnp.where((low_i == low_j) | (open_rows == 1), 0.0, MASKED)
     s["bars"][1] = jnp.where(top_i == top_j, 0.0, MASKED)
-    for copy in enter:
+    for copy in enter[:3]:
         copy.wait_recv()
 
-    cells = dot(order_ref[...], frame[:, :QUARTER, :].reshape(CELLS, PACK))
-    s["xs"][...] = cells[:, :C]
-    s["gm"][...] = cells[:, C:].astype(BF16)
+    s["xs"][...] = dot(order_ref[...], frame[:, :QUARTER, : 2 * 128].reshape(CELLS, 2 * 128))[:, :C]
 
     marks = jnp.concatenate(
         [
@@ -672,6 +675,10 @@
 
     lax.fori_loop(0, NWIN, forward, 0)
 
+    for copy in enter[3:]:
+        copy.wait_recv()
+    cells = dot(order_ref[...], frame[:, :QUARTER, 128:].reshape(CELLS, 2 * 128))
+    s["gm"][...] = cells[:, C - 128 :].astype(BF16)
     mixed = jnp.concatenate([dot_tn(s["ot"][w], w_proj[...]) for w in range(NWIN)], axis=0)
     mid = (s["xs"][...] + mixed).astype(BF16).astype(F32)
     n2, inv2 = normed_of(mid)
@@ -766,6 +773,7 @@
     late.z_start()
     early.z_back()
     table.z_back()
+    late.z_back()
     early.plane_back()
     table.pair_back()
     late.plane_back()
@@ -793,7 +801,7 @@
     vmem = pl.BlockSpec(memory_space=pltpu.VMEM)
     hbm = pl.BlockSpec(memory_space=pl.ANY)
     order = cell_order()
-    sums = (WeightSum(plan, ECOLS, False), WeightSum(plan, LCOLS, True), TableSum(plan))
+    sums = (WeightSum(plan, ECOLS, False), WeightSum(plan, LCOLS, False), TableSum(plan))
     consts = (
         order, order.T, table_lanes(0), table_lanes(1), table_sums(), column_of_cell(),
     )
@@ -801,7 +809,7 @@
     scratch = [pltpu.VMEM(v.shape, v.dtype) for v in far]
     scratch += [pltpu.VMEM(shape, dtype) for shape, dtype in SCRATCH.values()]
     sem = pltpu.SemaphoreType.DMA
-    scratch += [sem((len(FAR),)), sem((3,)), sem((3,)), sem((3,)), sem((3,)), sem((3,))]
+    scratch += [sem((len(FAR),)), sem((6,)), sem((6,)), sem((3,)), sem((3,)), sem((3,))]
     for one in sums:
         scratch += one.scratch()
     rows = lambda v: v.transpose(1, 0, 2).reshape(WH * LEVELS, WW * C)

time: 80.6 us -> 78.4 us (0.973)
  Pallas kernels: 79.7 us -> 77.6 us
    pallas_call x1, Pallas kernels: 76.7 us -> 74.5 us  [block(): pl.pallas_call(functools.partial(block_kernel, plan, sums), out_shape=[ja...]
where the time goes in v4:
time: 78.4 us; the launch traced here: 78.2 us
  Pallas kernels  77.6 us (99%)
    pallas_call x1, Pallas kernels, block(): pl.pallas_call(functools.partial(block_kernel, plan, sums), out_shape=[ja...  74.5 us
    pallas_call x1, Pallas kernels, write(): pl.pallas_call(functools.partial(write_kernel, plan, factor), out_shape=(...  3.05 us

profile of v4, /device:TPU:1, one launch (start us, length us, event | category | flops | bytes accessed | tf_op | source)
XLA Modules:
  0.0 78.2 jit_solution(8445199261715260649)
XLA Ops:
  0.6 74.5 %block.1 = (bf16[4,144,192]{2,1,0:T(8,128)(2,1)}, bf16[2,16,4,16,128]{4,3,2,1,0:T(8,128)(2,1)}, bf16[2,16,3,16,128]{4,3,2,1,0:T(8,128)(2,1)}, bf16[2,2,14,16,128]{4,3,2,1,0:T(8,128)(2,1)}) custom-call(bf16[48,2304]{1,0:T(8,128)(2,1)} %bitcast.13, bf16[48,2304]{1,0:T(8,128)(2,1)} %bitcast.14, s32[1,12]{1,0:T(1,128)} %bitcast.15, ...), custom_call_target="tpu_custom_call" | custom-call | tf_op jit(solution)/shard_map/block/pallas_call | solution.py:816
  75.2 3.1 %write.1 = (bf16[48,2304]{1,0:T(8,128)(2,1)}, f32[192,576]{1,0:T(8,128)}, f32[192,192]{1,0:T(8,128)}, f32[192,768]{1,0:T(8,128)}, f32[192,768]{1,0:T(8,128)}, /*index=5*/f32[4,19872]{1,0:T(4,128)}) custom-call(bf16[4,144,192]{2,1,0:T(8,128)(2,1)} %get-tuple-element.16.home_ref, bf16[2,16,4,16,128]{4,3,2,1,0:T(8,128)(2,1)} %get-tuple-element.17.early_ref, ...), custom_call_target="tpu_custom_call" | custom-call | tf_op jit(solution)/shard_map/write/pallas_call | solution.py:875
